TPU v7x, 32 devices: a whole 2x2x4 slice. The times are simulated.
32 devices in a mesh: segment: 4 (over y, x), dp: 8 (over z, core).
Axes of the slice: x: 2, y: 2, z: 4, core: 2. Of those that a mesh axis runs over, the one named last changes fastest.
Arguments:
- fwd_in: bfloat16 [2, 4, 8, 16, 32, 256], P(None, 'segment', 'dp'), may hold values from -6 to 6
- bwd_in: bfloat16 [4, 4, 8, 16, 32, 256], P(None, 'segment', 'dp'), may hold values from -6 to 6
- fresh: bfloat16 [2, 8, 16, 32, 256], P(None, 'dp'), may hold values from -6 to 6
- top_cot: bfloat16 [2, 8, 16, 32, 256], P(None, 'dp'), may hold values from -6 to 6
- conv_weight: bfloat16 [4, 256, 9, 256], P('segment', 'dp'), may hold values from -0.125 to 0.125
Outputs:
- fwd_out: bfloat16 [2, 4, 8, 16, 32, 256], P(None, 'segment', 'dp')
- bwd_out: bfloat16 [4, 4, 8, 16, 32, 256], P(None, 'segment', 'dp')
- weight_grad: float32 [4, 256, 9, 256], P('segment', 'dp')
All inputs are finite; a program needn't handle non-finite values.
Results may differ from a plain program's by a relative error of at most 0.0055.
Values may be sent and summed in bfloat16 or wider, within the bound.
No kernel may reach another device: no remote copies, remote signals or barrier semaphores. Data moves between devices by JAX's collectives and lax.ppermute only.
A program may use at most 64 MiB of HBM per device.

v0:
```python
import functools

import jax
import jax.numpy as jnp
from jax import lax
from jax.experimental import pallas as pl
from jax.experimental.pallas import tpu as pltpu
from jax.sharding import PartitionSpec as P

BF16 = jnp.bfloat16
F32 = jnp.float32
VMEM = pl.BlockSpec(memory_space=pltpu.VMEM)
SMEM = pl.BlockSpec(memory_space=pltpu.SMEM)
TAPS = 9
PARITY, FIRST, LAST, PLACE = range(4)
X2, Y1, G2, X1, Y2, G1, FRESH, TOP, LINES = 0, 2, 4, 6, 7, 8, 9, 10, 11
DIRECT = (2, 4, 8)
STEP_TWO = 3
COLLECT = 0
GRAD_ONE = 3


def call(kernel, out_shape, operands, weight=0, scratch=(), limit=32):
    name = getattr(kernel, "func", kernel).__name__
    return pl.pallas_call(
        kernel,
        name=name,
        out_shape=out_shape,
        in_specs=[SMEM] + [VMEM] * (len(operands) - 1),
        out_specs=jax.tree.map(lambda _: VMEM, out_shape),
        scratch_shapes=list(scratch),
        compiler_params=pltpu.CompilerParams(vmem_limit_bytes=limit * 1024 * 1024),
        cost_estimate=pl.CostEstimate(flops=int(weight), bytes_accessed=1, transcendentals=0),
    )(*operands)


def swapped(x, bit, name="halves"):
    with jax.named_scope(name):
        return lax.ppermute(x, "dp", [(i, i ^ bit) for i in range(lax.axis_size("dp"))])


def passed_along(block, distance, name):
    devices = range(lax.axis_size("segment"))
    route = [(i - distance, i) for i in devices if i - distance in devices]
    with jax.named_scope(name):
        return lax.ppermute(block, "segment", route)


def after(x, *others):
    return lax.optimization_barrier((x, *others))[0]


def flat(tile):
    return tile.reshape(-1, tile.shape[-1])


def unfold(ext, tile, near, beyond, parity, relu):
    width, channels = near.shape
    blank = jnp.zeros_like(near)
    around = [near] if beyond is None else [near, beyond]
    above = [jnp.where(parity == 1, line, blank) for line in around[::-1]]
    below = [jnp.where(parity == 0, line, blank) for line in around]
    rows = jnp.concatenate(above + [flat(tile)] + below, axis=0)
    if relu:
        rows = jnp.maximum(rows, jnp.zeros_like(rows))
    amount = rows.shape[0]
    wide = rows.astype(F32)
    col = lax.rem(lax.broadcasted_iota(jnp.int32, wide.shape, 0), width)
    left = jnp.where(col == 0, 0.0, pltpu.roll(wide, 1, 0))
    right = jnp.where(col == width - 1, 0.0, pltpu.roll(wide, amount - 1, 0))
    ext[:amount, :channels] = left.astype(BF16)
    ext[:amount, channels : 2 * channels] = rows
    ext[:amount, 2 * channels :] = right.astype(BF16)


def windows(ext, height, width):
    return jnp.concatenate([ext[a * width : (a + height) * width, :] for a in range(3)], axis=1)


def windows_and_near(ext, height, width, parity):
    parts = []
    for a in range(3):
        upper = ext[a * width : (a + 1) * width, :]
        lower = ext[(height + 1 + a) * width : (height + 2 + a) * width, :]
        inside = ext[(a + 1) * width : (a + 1 + height) * width, :]
        parts.append(jnp.concatenate([inside, jnp.where(parity == 0, lower, upper)], axis=0))
    return jnp.concatenate(parts, axis=1)


def conv(wide, weight):
    return jnp.dot(wide, weight[...].reshape(-1, weight.shape[2]), preferred_element_type=F32)


def conv_transposed(wide, weight):
    turned = jnp.concatenate([weight[TAPS - 1 - t] for t in range(TAPS)], axis=1)
    return lax.dot_general(wide, turned, (((1,), (1,)), ((), ())), preferred_element_type=F32)


def grad_into(store, stream, wide):
    lines = flat(stream)
    turned = jnp.maximum(lines, jnp.zeros_like(lines)).astype(F32).T.astype(BF16)
    outs = wide.shape[1] // TAPS
    for t in range(TAPS):
        other = TAPS - 1 - t
        store(t, jnp.dot(turned, wide[:, other * outs : (other + 1) * outs], preferred_element_type=F32))


def storing(info, outs, add):
    if len(outs) == 1:

        def store(t, total):
            outs[0][t] = total + outs[0][t] if add else total

        return store
    keep, give = outs

    def store_halves(t, total):
        parts, _, rows, channels = keep.shape
        cut = total.reshape(parts, 2, rows, channels)
        mine = jnp.where(info[PARITY] == 0, cut[:, 0], cut[:, 1])
        theirs = jnp.where(info[PARITY] == 0, cut[:, 1], cut[:, 0])
        if add:
            mine = mine + keep[:, t]
            theirs = theirs + give[:, t].astype(F32)
        keep[:, t] = mine
        give[:, t] = theirs.astype(BF16)

    return store_halves


def collect_kernel(info, fwd_in, bwd_in, fresh, top_cot, lines, early_fwd, early_back):
    parity = info[PARITY]

    def put(slot, tile, amount):
        height = tile.shape[0]
        for i in range(amount):
            lines[slot + i] = jnp.where(parity == 0, tile[height - 1 - i], tile[i])

    put(X2, fwd_in.at[1, 0, 0], 2)
    put(Y1, bwd_in.at[0, 0, 0], 2)
    put(G2, bwd_in.at[3, 0, 0], 2)
    put(X1, fwd_in.at[0, 0, 0], 1)
    put(Y2, bwd_in.at[1, 0, 0], 1)
    put(G1, bwd_in.at[2, 0, 0], 1)
    put(FRESH, fresh.at[1, 0], 1)
    put(TOP, top_cot.at[1, 0], 1)
    early_back[0] = bwd_in[0, 0, 0]
    early_back[1] = bwd_in[3, 0, 0]
    early_fwd[...] = fwd_in[1, 0, 0]


def grad_one_kernel(info, lines, fwd_in, bwd_in, top_cot, *rest):
    *outs, ext = rest
    height, width = fwd_in.shape[3:5]
    unfold(ext, bwd_in[3, 0, 0], lines[G2], None, info[PARITY], False)
    grad_into(storing(info, outs, False), bwd_in[0, 0, 0], windows(ext, height, width))

    @pl.when(info[LAST] == 1)
    def _():
        unfold(ext, top_cot[1, 0], lines[TOP], None, info[PARITY], False)
        grad_into(storing(info, outs, True), fwd_in[1, 0, 0], windows(ext, height, width))


def pair_sum_kernel(info, keep, got, stay, send):
    place = info[PLACE]
    for k in range(stay.shape[0]):
        here, there = lax.bitwise_xor(place, 2 * k), lax.bitwise_xor(place, 2 * k + 1)
        stay[k] = keep[here] + got[here].astype(F32)
        send[k] = (keep[there] + got[there].astype(F32)).astype(BF16)


def fold_kernel(info, held, got, stay, send):
    for k in range(stay.shape[0]):
        stay[k] = held[2 * k] + got[2 * k].astype(F32)
        send[k] = (held[2 * k + 1] + got[2 * k + 1].astype(F32)).astype(BF16)


def grown(tile, line):
    return jnp.concatenate([flat(tile), line], axis=0)


def step_one_kernel(info, lines, fwd_in, bwd_in, *rest):
    *pieces, message, second, weight, ext = rest
    height, width = bwd_in.shape[3:5]
    parity = info[PARITY]
    if len(pieces) == 1:
        weight[...] = pieces[0][...]
    else:
        rows = pieces[0].shape[1]
        half = len(pieces) // 2
        for k in range(half):
            there = 2 * lax.bitwise_xor(info[PLACE], k)
            for piece, slot in ((pieces[k], there + parity), (pieces[half + k], there + 1 - parity)):
                weight[:, pl.ds(pl.multiple_of(slot * rows, rows), rows), :] = piece[...]
    first_out = bwd_in[0, 0, 0]
    unfold(ext, first_out, lines[Y1], lines[Y1 + 1], parity, True)
    branch = conv(windows_and_near(ext, height, width, parity), weight)
    message[0] = (grown(bwd_in[1, 0, 0], lines[Y2]).astype(F32) - branch).astype(BF16)
    unfold(ext, bwd_in[3, 0, 0], lines[G2], lines[G2 + 1], parity, False)
    through = conv_transposed(windows_and_near(ext, height, width, parity), weight)
    kept = jnp.where(grown(first_out, lines[Y1]).astype(F32) > 0, through, 0.0)
    message[1] = (grown(bwd_in[2, 0, 0], lines[G1]).astype(F32) + kept).astype(BF16)
    unfold(ext, fwd_in[1, 0, 0], lines[X2], lines[X2 + 1], parity, True)
    branch = conv(windows_and_near(ext, height, width, parity), weight)
    second[...] = (grown(fwd_in[0, 0, 0], lines[X1]).astype(F32) + branch).astype(BF16)


def grad_two_kernel(height, width, info, message, *rest):
    *outs, ext = rest
    amount = height * width
    unfold(ext, message[1, :amount], message[1, amount:], None, info[PARITY], False)
    grad_into(storing(info, outs, False), message[0, :amount], windows(ext, height, width))


def forward_two_kernel(info, lines, early, second, fresh, weight, out, ext):
    height, width = fresh.shape[2:4]
    amount = height * width
    shape = early.shape
    first = info[FIRST] == 1
    stream = jnp.where(first, flat(fresh[1, 0]), second[:amount])
    near = jnp.where(first, lines[FRESH], second[amount:])
    unfold(ext, stream, near, None, info[PARITY], True)
    out[0, 0, 0] = stream.reshape(shape)
    other = jnp.where(first, fresh[0, 0], early[...])
    branch = conv(windows(ext, height, width), weight).reshape(shape)
    out[1, 0, 0] = (other.astype(F32) + branch).astype(BF16)


def backward_two_kernel(info, lines, early, message, own_second, fwd_in, top_cot, weight, out, ext):
    height, width = top_cot.shape[2:4]
    amount = height * width
    shape = early.shape[1:]
    last = info[LAST] == 1
    out_first = jnp.where(last, flat(fwd_in[1, 0, 0]), message[0, :amount])
    near = jnp.where(last, lines[X2], message[0, amount:])
    out[1, 0, 0] = out_first.reshape(shape)
    unfold(ext, out_first, near, None, info[PARITY], True)
    out_second = jnp.where(last, own_second[:amount], flat(early[0])).reshape(shape)
    branch = conv(windows(ext, height, width), weight).reshape(shape)
    out[0, 0, 0] = (out_second.astype(F32) - branch).astype(BF16)
    cot_second = jnp.where(last, flat(top_cot[1, 0]), message[1, :amount])
    near = jnp.where(last, lines[TOP], message[1, amount:])
    out[2, 0, 0] = cot_second.reshape(shape)
    unfold(ext, cot_second, near, None, info[PARITY], False)
    through = conv_transposed(windows(ext, height, width), weight).reshape(shape)
    cot_first = jnp.where(last, top_cot[0, 0], early[1])
    kept = jnp.where(out[1, 0, 0].astype(F32) > 0, through, 0.0)
    out[3, 0, 0] = (cot_first.astype(F32) + kept).astype(BF16)


def summed(own, parts):
    return functools.reduce(lambda x, y: x + y, [own[...]] + [p[...].astype(F32) for p in parts])


def gather_sum_kernel(info, own, *rest):
    *parts, out = rest
    out[...] = summed(own, parts).astype(BF16)


def finish_kernel(scale, info, own, *rest):
    *parts, out = rest
    out[...] = summed(own, parts) * scale


def shards(fwd_in, bwd_in, fresh, top_cot, conv_weight):
    dp = lax.axis_size("dp")
    places = dp // 2
    dp_pos = lax.axis_index("dp")
    segment_pos = lax.axis_index("segment")
    height, width, channels = fwd_in.shape[3:]
    shard = conv_weight[0].transpose(1, 0, 2)
    rows = shard.shape[1]
    outs = shard.shape[2]
    direct = places in DIRECT and rows % 16 == 0
    info = jnp.stack(
        [
            dp_pos % 2,
            (segment_pos == 0).astype(jnp.int32),
            (segment_pos == lax.axis_size("segment") - 1).astype(jnp.int32),
            dp_pos // 2,
        ]
    ).astype(jnp.int32)
    like = lambda x, dtype: jax.ShapeDtypeStruct(x.shape, dtype)
    taller = lambda *lead: jax.ShapeDtypeStruct(lead + ((height + 1) * width, channels), BF16)
    ext = pltpu.VMEM(((height + 4) * width, 3 * channels), BF16)
    conv_flops = 2 * height * width * channels * TAPS * outs

    if direct:
        mine = [shard]
        for k in range(1, places):
            low = k & -k
            mine.append(swapped(mine[k - low], 2 * low, "weight_z%d" % k))

    tile = lambda *lead: jax.ShapeDtypeStruct(lead + (height, width, channels), BF16)
    lines, early_fwd, early_back = call(
        collect_kernel,
        (jax.ShapeDtypeStruct((LINES, width, channels), BF16), tile(), tile(2)),
        (info, fwd_in, bwd_in, fresh, top_cot),
        COLLECT * conv_flops,
        limit=60,
    )
    lines = swapped(lines, 1, "lines")
    early_back = passed_along(early_back, -1, "early_back")

    def grads(kernel, operands, weight):
        if not direct:
            return call(kernel, (jax.ShapeDtypeStruct((TAPS, channels, outs), F32),), operands, weight, [ext])
        split = (places, TAPS, rows, outs)
        shape = (jax.ShapeDtypeStruct(split, F32), jax.ShapeDtypeStruct(split, BF16))
        return call(kernel, shape, operands, weight, [ext])

    def scattered(name, keep, give=None, hold=()):
        if not direct:
            return lax.psum_scatter(keep, "dp", scatter_dimension=1, tiled=True), []
        amount = places // 2
        shape = lambda dtype: jax.ShapeDtypeStruct((amount,) + shard.shape, dtype)
        got = swapped(give, 1, name)
        stay, send = call(pair_sum_kernel, (shape(F32), shape(BF16)), (after(info, *hold[:1]), keep, got))
        bit = 2
        while amount > 1:
            got = swapped(send, bit, name + "_near")
            amount, bit = amount // 2, 2 * bit
            stay, send = call(fold_kernel, (shape(F32), shape(BF16)), (after(info, *hold[1:]), stay, got))
        return stay[0], [swapped(send, bit, name + "_far")[0]]

    terms_one = grads(grad_one_kernel, (info, lines, fwd_in, bwd_in, top_cot), GRAD_ONE * conv_flops)
    if direct:
        others = mine[:-1] + [after(mine[-1], terms_one[0])]
        pieces = mine + [swapped(x, 1, "weight_core%d" % k) for k, x in enumerate(others)]
        early_fwd = after(early_fwd, pieces[-2])
    else:
        pieces = [lax.all_gather(shard, "dp", axis=1, tiled=True)]

    early_fwd = passed_along(early_fwd, 1, "early_fwd")

    message, second, weight = call(
        step_one_kernel,
        (taller(2), taller(), jax.ShapeDtypeStruct((TAPS, channels, outs), BF16)),
        (after(info, early_back), lines, fwd_in, bwd_in, *pieces),
        1,
        [ext],
    )
    late_back = passed_along(message, -1, "late_back")
    late_fwd = passed_along(second, 1, "late_fwd")

    terms_two = grads(functools.partial(grad_two_kernel, height, width), (after(info, early_fwd), message), 1)
    own_one, parts_one = scattered("term_one", *terms_one)
    own_two, parts_two = scattered("term_two", *terms_two)
    below = call(gather_sum_kernel, like(shard, BF16), (info, own_two, *parts_two))
    from_above = passed_along(below, -1, "below")

    fwd_out = call(
        forward_two_kernel,
        like(fwd_in, BF16),
        (info, lines, early_fwd, late_fwd, fresh, weight),
        STEP_TWO * conv_flops,
        [ext],
    )
    bwd_out = call(
        backward_two_kernel,
        like(bwd_in, BF16),
        (info, lines, early_back, late_back, second, fwd_in, top_cot, weight),
        STEP_TWO * conv_flops,
        [ext],
    )
    scale = (2.0 * dp * height * width) ** -0.5
    finish = functools.partial(finish_kernel, scale)
    grad = call(finish, like(shard, F32), (info, own_one, *parts_one, from_above))
    return fwd_out, bwd_out, grad.transpose(1, 0, 2)[None]


def solution(mesh):
    in_specs = (
        P(None, "segment", "dp", None, None, None),
        P(None, "segment", "dp", None, None, None),
        P(None, "dp", None, None, None),
        P(None, "dp", None, None, None),
        P("segment", "dp", None, None),
    )
    out_specs = (
        P(None, "segment", "dp", None, None, None),
        P(None, "segment", "dp", None, None, None),
        P("segment", "dp", None, None),
    )
    return jax.shard_map(shards, mesh=mesh, in_specs=in_specs, out_specs=out_specs, check_vma=False)
```

profile of v0, /device:TPU:7, one launch (start us, length us, event | category | flops | bytes accessed | tf_op | source)
XLA Modules:
  0.0 66.6 jit_solution(6794874658959744354)
XLA Ops:
  0.6 2.4 %collective-permute-start.1 = (bf16[9,32,256]{2,1,0:T(8,128)(2,1)}, bf16[9,32,256]{2,1,0:T(8,128)(2,1)S(1)}, u32[]{:S(2)}, u32[]{:S(2)}) collective-permute-start(bf16[9,32,256]{2,1,0:T(8,128)(2,1)} %bitcast.16), channel_id=1, source_target_pairs={{0,4},{1,5},{2,6},{3,7},{4,0},{5,1},{6,2},{7,3},{8,12},{9,13},{10,... | collective-permute-start | bytes 442376 | tf_op jit(solution)/shard_map/weight_z2/ppermute | solution.py:39
  3.0 0.7 pad_add_fusion.info
  3.7 0.0 copy-start.4
  3.7 0.0 copy-start
  3.7 0.0 copy-start.1
  3.7 0.0 copy-start.3
  3.7 0.0 copy-start.5
  3.7 2.8 %collect_kernel.1 = (bf16[11,32,256]{2,1,0:T(8,128)(2,1)}, bf16[16,32,256]{2,1,0:T(8,128)(2,1)}, bf16[2,16,32,256]{3,2,1,0:T(8,128)(2,1)}) custom-call(s32[4]{0:T(128)} %pad_add_fusion.info, bf16[2,1,1,16,32,256]{5,4,3,2,1,0:T(8,128)(2,1)} %fwd_in.7, bf16[4,1,1,16,32,256]{5,4,3,2,1,0:T(8,128)(2,1)} %bwd_in.5, bf16[2,1,16,32,256]{4,3,2,1,0:T(8,128)(2,1)} %fresh.3, ...), custom_call_target="tpu_custom_call" | custom-call | bytes 1 | tf_op jit(solution)/shard_map/collect_kernel/pallas_call | solution.py:25
  6.5 2.2 %collective-permute-start.4 = (bf16[2,16,32,256]{3,2,1,0:T(8,128)(2,1)}, bf16[2,16,32,256]{3,2,1,0:T(8,128)(2,1)S(1)}, u32[]{:S(2)}, u32[]{:S(2)}) collective-permute-start(bf16[2,16,32,256]{3,2,1,0:T(8,128)(2,1)} %get-tuple-element.28), channel_id=1, source_target_pairs={{8,0},{16,8},{24,16},{9,1},{17,9},{25,17},{10,2},{18,10},{26,18},{... | collective-permute-start | bytes 1572872 | tf_op jit(solution)/shard_map/early_back/ppermute | solution.py:46
  8.7 1.3 %collective-permute-start = (bf16[11,32,256]{2,1,0:T(8,128)(2,1)}, bf16[11,32,256]{2,1,0:T(8,128)(2,1)S(1)}, u32[]{:S(2)}, u32[]{:S(2)}) collective-permute-start(bf16[11,32,256]{2,1,0:T(8,128)(2,1)} %get-tuple-element.25), channel_id=1, source_target_pairs={{0,1},{1,0},{2,3},{3,2},{4,5},{5,4},{6,7},{7,6},{8,9},{9,8},{10,11... | collective-permute-start | bytes 540680 | tf_op jit(solution)/shard_map/lines/ppermute | solution.py:39
  10.0 0.0 copy-done.4
  10.0 1.3 %collective-permute-start.5 = (bf16[9,32,256]{2,1,0:T(8,128)(2,1)S(1)}, bf16[9,32,256]{2,1,0:T(8,128)(2,1)S(1)}, u32[]{:S(2)}, u32[]{:S(2)}) collective-permute-start(bf16[9,32,256]{2,1,0:T(8,128)(2,1)S(1)} %bitcast.17), channel_id=1, source_target_pairs={{0,2},{1,3},{2,0},{3,1},{4,6},{5,7},{6,4},{7,5},{8,10},{9,11},{10,... | collective-permute-start | bytes 442376 | tf_op jit(solution)/shard_map/weight_z1/ppermute | solution.py:39
  11.3 0.0 collective-permute-done.1.rest_2_
  11.3 0.4 collective-permute-start.2
  11.6 0.2 collective-permute-start.7
  11.8 3.6 %collective-permute-done.5.rest_1_ = bf16[9,32,256]{2,1,0:T(8,128)(2,1)S(1)} collective-permute-done((bf16[9,32,256]{2,1,0:T(8,128)(2,1)S(1)}, bf16[9,32,256]{2,1,0:T(8,128)(2,1)S(1)}, u32[]{:S(2)}, u32[]{:S(2)}) %collective-permute-start.5) | collective-permute-done | bytes 147488 | tf_op jit(solution)/shard_map/weight_z1/ppermute | solution.py:39
  15.4 1.3 %collective-permute-start.6 = (bf16[9,32,256]{2,1,0:T(8,128)(2,1)S(1)}, bf16[9,32,256]{2,1,0:T(8,128)(2,1)S(1)}, u32[]{:S(2)}, u32[]{:S(2)}) collective-permute-start(bf16[9,32,256]{2,1,0:T(8,128)(2,1)S(1)} %collective-permute-done.1.rest_2_), channel_id=1, source_target_pairs={{0,2},{1,3},{2,0},{3,1},{4,6},{5,7},{6,4},{7,5},{8,10},{9,11},{10,... | collective-permute-start | bytes 442376 | tf_op jit(solution)/shard_map/weight_z3/ppermute | solution.py:39
  16.7 0.0 collective-permute-done.2.rest_6_
  16.7 1.1 %collective-permute-start.8 = (bf16[9,32,256]{2,1,0:T(8,128)(2,1)S(1)}, bf16[9,32,256]{2,1,0:T(8,128)(2,1)S(1)}, u32[]{:S(2)}, u32[]{:S(2)}) collective-permute-start(bf16[9,32,256]{2,1,0:T(8,128)(2,1)S(1)} %collective-permute-done.5.rest_1_), channel_id=1, source_target_pairs={{0,1},{1,0},{2,3},{3,2},{4,5},{5,4},{6,7},{7,6},{8,9},{9,8},{10,11... | collective-permute-start | bytes 442376 | tf_op jit(solution)/shard_map/weight_core1/ppermute | solution.py:39
  17.8 0.0 collective-permute-done.lines
  17.8 1.3 %collective-permute-start.3 = (bf16[16,32,256]{2,1,0:T(8,128)(2,1)}, bf16[16,32,256]{2,1,0:T(8,128)(2,1)S(1)}, u32[]{:S(2)}, u32[]{:S(2)}) collective-permute-start(bf16[16,32,256]{2,1,0:T(8,128)(2,1)} %get-tuple-element.27), channel_id=1, source_target_pairs={{0,8},{8,16},{16,24},{1,9},{9,17},{17,25},{2,10},{10,18},{18,26},{... | collective-permute-start | bytes 786440 | tf_op jit(solution)/shard_map/early_fwd/ppermute | solution.py:46
  19.1 0.0 copy-done
  19.1 0.0 copy-done.1
  19.1 0.0 copy-done.3
  19.1 0.0 copy-done.5
  19.2 2.4 %grad_one_kernel.1 = (f32[4,9,32,256]{3,2,1,0:T(8,128)S(1)}, bf16[4,9,32,256]{3,2,1,0:T(8,128)(2,1)S(1)}) custom-call(s32[4]{0:T(128)S(1)} %copy-done.5, bf16[11,32,256]{2,1,0:T(8,128)(2,1)S(1)} %collective-permute-done.lines, bf16[2,1,1,16,32,256]{5,4,3,2,1,0:T(8,128)(2,1)S(1)} %copy-done.1, bf16[4,1,1,16,32,256]{5,4,3,2,1,0:T(8,128)(2,1)S(1)} %copy-done, ...), custom_call_target="tpu_custom_call" | custom-call | flops 1811939328 | bytes 1 | tf_op jit(solution)/shard_map/grad_one_kernel/pallas_call | solution.py:25
  21.5 0.0 collective-permute-done.6.rest_3_
  21.5 0.1 collective-permute-start.9
  21.6 0.0 collective-permute-done.4.early
  21.6 0.0 collective-permute-done.7.rest_4_
  21.7 0.0 collective-permute-done.8.rest_5_
  21.7 1.3 %collective-permute-done.9.rest_7_ = bf16[9,32,256]{2,1,0:T(8,128)(2,1)S(1)} collective-permute-done((bf16[9,32,256]{2,1,0:T(8,128)(2,1)S(1)}, bf16[9,32,256]{2,1,0:T(8,128)(2,1)S(1)}, u32[]{:S(2)}, u32[]{:S(2)}) %collective-permute-start.9) | collective-permute-done | bytes 147488 | tf_op jit(solution)/shard_map/weight_core3/ppermute | solution.py:39
  23.0 2.9 %step_one_kernel.1 = (bf16[2,544,256]{2,1,0:T(8,128)(2,1)S(1)}, bf16[544,256]{1,0:T(8,128)(2,1)S(1)}, bf16[9,256,256]{2,1,0:T(8,128)(2,1)S(1)}) custom-call(s32[4]{0:T(128)S(1)} %copy-done.5, bf16[11,32,256]{2,1,0:T(8,128)(2,1)S(1)} %collective-permute-done.lines, bf16[2,1,1,16,32,256]{5,4,3,2,1,0:T(8,128)(2,1)S(1)} %copy-done.1, ...), custom_call_target="tpu_custom_call" | custom-call | flops 1 | bytes 1 | tf_op jit(solution)/shard_map/step_one_kernel/pallas_call | solution.py:25
  25.9 2.0 %collective-permute-done.3.early = bf16[16,32,256]{2,1,0:T(8,128)(2,1)S(1)} collective-permute-done((bf16[16,32,256]{2,1,0:T(8,128)(2,1)}, bf16[16,32,256]{2,1,0:T(8,128)(2,1)S(1)}, u32[]{:S(2)}, u32[]{:S(2)}) %collective-permute-start.3) | collective-permute-done | bytes 262176 | tf_op jit(solution)/shard_map/early_fwd/ppermute | solution.py:46
  27.8 1.4 %grad_two_kernel.1 = (f32[4,9,32,256]{3,2,1,0:T(8,128)S(1)}, bf16[4,9,32,256]{3,2,1,0:T(8,128)(2,1)S(1)}) custom-call(s32[4]{0:T(128)S(1)} %copy-done.5, bf16[2,544,256]{2,1,0:T(8,128)(2,1)S(1)} %get-tuple-element.34.message), custom_call_target="tpu_custom_call" | custom-call | flops 1 | bytes 1 | tf_op jit(solution)/shard_map/grad_two_kernel/pallas_call | solution.py:25
  29.3 0.9 %collective-permute-start.15 = (bf16[4,9,32,256]{3,2,1,0:T(8,128)(2,1)S(1)}, bf16[4,9,32,256]{3,2,1,0:T(8,128)(2,1)S(1)}, u32[]{:S(2)}, u32[]{:S(2)}) collective-permute-start(bf16[4,9,32,256]{3,2,1,0:T(8,128)(2,1)S(1)} %get-tuple-element.42), channel_id=1, source_target_pairs={{0,1},{1,0},{2,3},{3,2},{4,5},{5,4},{6,7},{7,6},{8,9},{9,8},{10,11... | collective-permute-start | bytes 1769480 | tf_op jit(solution)/shard_map/term_two/ppermute | solution.py:39
  30.1 0.1 collective-permute-start.12
  30.2 4.0 %collective-permute-start.11 = (bf16[2,544,256]{2,1,0:T(8,128)(2,1)S(1)}, bf16[2,544,256]{2,1,0:T(8,128)(2,1)S(1)}, u32[]{:S(2)}, u32[]{:S(2)}) collective-permute-start(bf16[2,544,256]{2,1,0:T(8,128)(2,1)S(1)} %get-tuple-element.34.message), channel_id=1, source_target_pairs={{8,0},{16,8},{24,16},{9,1},{17,9},{25,17},{10,2},{18,10},{26,18},{... | collective-permute-start | bytes 1671176 | tf_op jit(solution)/shard_map/late_back/ppermute | solution.py:46
  34.2 0.0 collective-permute-done.15.got
  34.2 0.6 pair_sum_kernel.3
  34.8 0.2 collective-permute-start.16
  35.1 0.0 copy-start.2
  35.1 1.4 %collective-permute-start.10 = (bf16[544,256]{1,0:T(8,128)(2,1)S(1)}, bf16[544,256]{1,0:T(8,128)(2,1)S(1)}, u32[]{:S(2)}, u32[]{:S(2)}) collective-permute-start(bf16[544,256]{1,0:T(8,128)(2,1)S(1)} %get-tuple-element.32.own_second), channel_id=1, source_target_pairs={{0,8},{8,16},{16,24},{1,9},{9,17},{17,25},{2,10},{10,18},{18,26},{... | collective-permute-start | bytes 835592 | tf_op jit(solution)/shard_map/late_fwd/ppermute | solution.py:46
  36.5 0.0 collective-permute-done.12.got
  36.5 0.6 pair_sum_kernel.2
  37.2 1.4 %collective-permute-start.13 = (bf16[2,9,32,256]{3,2,1,0:T(8,128)(2,1)S(1)}, bf16[2,9,32,256]{3,2,1,0:T(8,128)(2,1)S(1)}, u32[]{:S(2)}, u32[]{:S(2)}) collective-permute-start(bf16[2,9,32,256]{3,2,1,0:T(8,128)(2,1)S(1)} %get-tuple-element.37), channel_id=1, source_target_pairs={{0,2},{1,3},{2,0},{3,1},{4,6},{5,7},{6,4},{7,5},{8,10},{9,11},{10,... | collective-permute-start | bytes 884744 | tf_op jit(solution)/shard_map/term_one_near/ppermute | solution.py:39
  38.5 4.2 %collective-permute-done.16.got = bf16[2,9,32,256]{3,2,1,0:T(8,128)(2,1)S(1)} collective-permute-done((bf16[2,9,32,256]{3,2,1,0:T(8,128)(2,1)S(1)}, bf16[2,9,32,256]{3,2,1,0:T(8,128)(2,1)S(1)}, u32[]{:S(2)}, u32[]{:S(2)}) %collective-permute-start.16) | collective-permute-done | bytes 294944 | tf_op jit(solution)/shard_map/term_two_near/ppermute | solution.py:39
  42.7 0.6 fold_kernel.3
  43.3 0.1 collective-permute-start.17
  43.5 9.3 %collective-permute-done.10.second = bf16[544,256]{1,0:T(8,128)(2,1)S(1)} collective-permute-done((bf16[544,256]{1,0:T(8,128)(2,1)S(1)}, bf16[544,256]{1,0:T(8,128)(2,1)S(1)}, u32[]{:S(2)}, u32[]{:S(2)}) %collective-permute-start.10) | collective-permute-done | bytes 278560 | tf_op jit(solution)/shard_map/late_fwd/ppermute | solution.py:46
  52.7 0.0 copy-done.2
  52.7 2.2 %forward_two_kernel.1 = bf16[2,1,1,16,32,256]{5,4,3,2,1,0:T(8,128)(2,1)} custom-call(s32[4]{0:T(128)S(1)} %copy-done.5, bf16[11,32,256]{2,1,0:T(8,128)(2,1)S(1)} %collective-permute-done.lines, bf16[16,32,256]{2,1,0:T(8,128)(2,1)S(1)} %collective-permute-done.3.early, bf16[544,256]{1,0:T(8,128)(2,1)S(1)} %collective-permute-done.10.second, ...), custom_call_target="tpu_custom_call" | custom-call | flops 1811939328 | bytes 1 | tf_op jit(solution)/shard_map/forward_two_kernel/pallas_call | solution.py:25
  54.9 0.0 collective-permute-done.13.got
  54.9 0.6 fold_kernel.2
  55.5 0.1 collective-permute-start.14
  55.6 0.0 collective-permute-done.17
  55.6 0.6 gather_sum_kernel.1
  56.2 1.6 %collective-permute-start.18 = (bf16[9,32,256]{2,1,0:T(8,128)(2,1)S(1)}, bf16[9,32,256]{2,1,0:T(8,128)(2,1)S(1)}, u32[]{:S(2)}, u32[]{:S(2)}) collective-permute-start(bf16[9,32,256]{2,1,0:T(8,128)(2,1)S(1)} %gather_sum_kernel.1), channel_id=1, source_target_pairs={{8,0},{16,8},{24,16},{9,1},{17,9},{25,17},{10,2},{18,10},{26,18},{... | collective-permute-start | bytes 442376 | tf_op jit(solution)/shard_map/below/ppermute | solution.py:46
  57.8 0.0 collective-permute-done.11.message
  57.8 3.0 %backward_two_kernel.1 = bf16[4,1,1,16,32,256]{5,4,3,2,1,0:T(8,128)(2,1)} custom-call(s32[4]{0:T(128)S(1)} %copy-done.5, bf16[11,32,256]{2,1,0:T(8,128)(2,1)S(1)} %collective-permute-done.lines, bf16[2,16,32,256]{3,2,1,0:T(8,128)(2,1)S(1)} %collective-permute-done.4.early, bf16[2,544,256]{2,1,0:T(8,128)(2,1)S(1)} %collective-permute-done.11.message, ...), custom_call_target="tpu_custom_call" | custom-call | flops 1811939328 | bytes 1 | tf_op jit(solution)/shard_map/backward_two_kernel/pallas_call | solution.py:25
  60.8 4.5 %collective-permute-done.14 = bf16[1,9,32,256]{3,2,1,0:T(8,128)(2,1)S(1)} collective-permute-done((bf16[1,9,32,256]{3,2,1,0:T(8,128)(2,1)S(1)}, bf16[1,9,32,256]{3,2,1,0:T(8,128)(2,1)S(1)}, u32[]{:S(2)}, u32[]{:S(2)}) %collective-permute-start.14) | collective-permute-done | bytes 147488 | tf_op jit(solution)/shard_map/term_one_far/ppermute | solution.py:39
  65.3 0.0 collective-permute-done.18.rest_1_
  65.3 1.3 %finish_kernel.1 = f32[9,32,256]{2,1,0:T(8,128)} custom-call(s32[4]{0:T(128)S(1)} %copy-done.5, f32[9,32,256]{2,1,0:T(8,128)S(1)} %bitcast.14, bf16[9,32,256]{2,1,0:T(8,128)(2,1)S(1)} %bitcast.20, bf16[9,32,256]{2,1,0:T(8,128)(2,1)S(1)} %collective-permute-done.18.rest_1_), custom_call_target="tpu_custom_call" | custom-call | bytes 1 | tf_op jit(solution)/shard_map/finish_kernel/pallas_call | solution.py:25
Async XLA Ops:
  0.6 10.6 %collective-permute-start.1 = (bf16[9,32,256]{2,1,0:T(8,128)(2,1)}, bf16[9,32,256]{2,1,0:T(8,128)(2,1)S(1)}, u32[]{:S(2)}, u32[]{:S(2)}) collective-permute-start(bf16[9,32,256]{2,1,0:T(8,128)(2,1)} %bitcast.16), channel_id=1, source_target_pairs={{0,4},{1,5},{2,6},{3,7},{4,0},{5,1},{6,2},{7,3},{8,12},{9,13},{10,... | collective-permute-start | bytes 442376 | tf_op jit(solution)/shard_map/weight_z2/ppermute | solution.py:39
  3.7 6.3 %copy-start.4 = (bf16[1,32,9,256]{3,1,2,0:T(8,128)(2,1)S(1)}, bf16[1,32,9,256]{3,1,2,0:T(8,128)(2,1)}, u32[]{:S(2)}) copy-start(bf16[1,32,9,256]{3,1,2,0:T(8,128)(2,1)} %param.9) | copy-start | bytes 442372
  3.7 15.5 %copy-start = (bf16[4,1,1,16,32,256]{5,4,3,2,1,0:T(8,128)(2,1)S(1)}, bf16[4,1,1,16,32,256]{5,4,3,2,1,0:T(8,128)(2,1)}, u32[]{:S(2)}) copy-start(bf16[4,1,1,16,32,256]{5,4,3,2,1,0:T(8,128)(2,1)} %bwd_in.5) | copy-start | bytes 3145732
  3.7 15.5 %copy-start.1 = (bf16[2,1,1,16,32,256]{5,4,3,2,1,0:T(8,128)(2,1)S(1)}, bf16[2,1,1,16,32,256]{5,4,3,2,1,0:T(8,128)(2,1)}, u32[]{:S(2)}) copy-start(bf16[2,1,1,16,32,256]{5,4,3,2,1,0:T(8,128)(2,1)} %fwd_in.7) | copy-start | bytes 1572868
  3.7 15.5 %copy-start.3 = (bf16[2,1,16,32,256]{4,3,2,1,0:T(8,128)(2,1)S(1)}, bf16[2,1,16,32,256]{4,3,2,1,0:T(8,128)(2,1)}, u32[]{:S(2)}) copy-start(bf16[2,1,16,32,256]{4,3,2,1,0:T(8,128)(2,1)} %top_cot.5) | copy-start | bytes 1572868
  3.7 15.5 %copy-start.5 = (s32[4]{0:T(128)S(1)}, s32[4]{0:T(128)}, u32[]{:S(2)}) copy-start(s32[4]{0:T(128)} %pad_add_fusion.info) | copy-start | bytes 52
  6.5 15.2 %collective-permute-start.4 = (bf16[2,16,32,256]{3,2,1,0:T(8,128)(2,1)}, bf16[2,16,32,256]{3,2,1,0:T(8,128)(2,1)S(1)}, u32[]{:S(2)}, u32[]{:S(2)}) collective-permute-start(bf16[2,16,32,256]{3,2,1,0:T(8,128)(2,1)} %get-tuple-element.28), channel_id=1, source_target_pairs={{8,0},{16,8},{24,16},{9,1},{17,9},{25,17},{10,2},{18,10},{26,18},{... | collective-permute-start | bytes 1572872 | tf_op jit(solution)/shard_map/early_back/ppermute | solution.py:46
  8.7 9.2 %collective-permute-start = (bf16[11,32,256]{2,1,0:T(8,128)(2,1)}, bf16[11,32,256]{2,1,0:T(8,128)(2,1)S(1)}, u32[]{:S(2)}, u32[]{:S(2)}) collective-permute-start(bf16[11,32,256]{2,1,0:T(8,128)(2,1)} %get-tuple-element.25), channel_id=1, source_target_pairs={{0,1},{1,0},{2,3},{3,2},{4,5},{5,4},{6,7},{7,6},{8,9},{9,8},{10,11... | collective-permute-start | bytes 540680 | tf_op jit(solution)/shard_map/lines/ppermute | solution.py:39
  10.0 5.4 %collective-permute-start.5 = (bf16[9,32,256]{2,1,0:T(8,128)(2,1)S(1)}, bf16[9,32,256]{2,1,0:T(8,128)(2,1)S(1)}, u32[]{:S(2)}, u32[]{:S(2)}) collective-permute-start(bf16[9,32,256]{2,1,0:T(8,128)(2,1)S(1)} %bitcast.17), channel_id=1, source_target_pairs={{0,2},{1,3},{2,0},{3,1},{4,6},{5,7},{6,4},{7,5},{8,10},{9,11},{10,... | collective-permute-start | bytes 442376 | tf_op jit(solution)/shard_map/weight_z1/ppermute | solution.py:39
  11.3 5.4 %collective-permute-start.2 = (bf16[9,32,256]{2,1,0:T(8,128)(2,1)S(1)}, bf16[9,32,256]{2,1,0:T(8,128)(2,1)S(1)}, u32[]{:S(2)}, u32[]{:S(2)}) collective-permute-start(bf16[9,32,256]{2,1,0:T(8,128)(2,1)S(1)} %collective-permute-done.1.rest_2_), channel_id=1, source_target_pairs={{0,1},{1,0},{2,3},{3,2},{4,5},{5,4},{6,7},{7,6},{8,9},{9,8},{10,11... | collective-permute-start | bytes 442376 | tf_op jit(solution)/shard_map/weight_core2/ppermute | solution.py:39
  11.6 10.0 %collective-permute-start.7 = (bf16[9,32,256]{2,1,0:T(8,128)(2,1)S(1)}, bf16[9,32,256]{2,1,0:T(8,128)(2,1)S(1)}, u32[]{:S(2)}, u32[]{:S(2)}) collective-permute-start(bf16[9,32,256]{2,1,0:T(8,128)(2,1)S(1)} %bitcast.18), channel_id=1, source_target_pairs={{0,1},{1,0},{2,3},{3,2},{4,5},{5,4},{6,7},{7,6},{8,9},{9,8},{10,11... | collective-permute-start | bytes 442376 | tf_op jit(solution)/shard_map/weight_core0/ppermute | solution.py:39
  15.4 6.2 %collective-permute-start.6 = (bf16[9,32,256]{2,1,0:T(8,128)(2,1)S(1)}, bf16[9,32,256]{2,1,0:T(8,128)(2,1)S(1)}, u32[]{:S(2)}, u32[]{:S(2)}) collective-permute-start(bf16[9,32,256]{2,1,0:T(8,128)(2,1)S(1)} %collective-permute-done.1.rest_2_), channel_id=1, source_target_pairs={{0,2},{1,3},{2,0},{3,1},{4,6},{5,7},{6,4},{7,5},{8,10},{9,11},{10,... | collective-permute-start | bytes 442376 | tf_op jit(solution)/shard_map/weight_z3/ppermute | solution.py:39
  16.7 5.0 %collective-permute-start.8 = (bf16[9,32,256]{2,1,0:T(8,128)(2,1)S(1)}, bf16[9,32,256]{2,1,0:T(8,128)(2,1)S(1)}, u32[]{:S(2)}, u32[]{:S(2)}) collective-permute-start(bf16[9,32,256]{2,1,0:T(8,128)(2,1)S(1)} %collective-permute-done.5.rest_1_), channel_id=1, source_target_pairs={{0,1},{1,0},{2,3},{3,2},{4,5},{5,4},{6,7},{7,6},{8,9},{9,8},{10,11... | collective-permute-start | bytes 442376 | tf_op jit(solution)/shard_map/weight_core1/ppermute | solution.py:39
  17.8 10.0 %collective-permute-start.3 = (bf16[16,32,256]{2,1,0:T(8,128)(2,1)}, bf16[16,32,256]{2,1,0:T(8,128)(2,1)S(1)}, u32[]{:S(2)}, u32[]{:S(2)}) collective-permute-start(bf16[16,32,256]{2,1,0:T(8,128)(2,1)} %get-tuple-element.27), channel_id=1, source_target_pairs={{0,8},{8,16},{16,24},{1,9},{9,17},{17,25},{2,10},{10,18},{18,26},{... | collective-permute-start | bytes 786440 | tf_op jit(solution)/shard_map/early_fwd/ppermute | solution.py:46
  21.5 1.4 %collective-permute-start.9 = (bf16[9,32,256]{2,1,0:T(8,128)(2,1)S(1)}, bf16[9,32,256]{2,1,0:T(8,128)(2,1)S(1)}, u32[]{:S(2)}, u32[]{:S(2)}) collective-permute-start(bf16[9,32,256]{2,1,0:T(8,128)(2,1)S(1)} %collective-permute-done.6.rest_3_), channel_id=1, source_target_pairs={{0,1},{1,0},{2,3},{3,2},{4,5},{5,4},{6,7},{7,6},{8,9},{9,8},{10,11... | collective-permute-start | bytes 442376 | tf_op jit(solution)/shard_map/weight_core3/ppermute | solution.py:39
  29.3 4.9 %collective-permute-start.15 = (bf16[4,9,32,256]{3,2,1,0:T(8,128)(2,1)S(1)}, bf16[4,9,32,256]{3,2,1,0:T(8,128)(2,1)S(1)}, u32[]{:S(2)}, u32[]{:S(2)}) collective-permute-start(bf16[4,9,32,256]{3,2,1,0:T(8,128)(2,1)S(1)} %get-tuple-element.42), channel_id=1, source_target_pairs={{0,1},{1,0},{2,3},{3,2},{4,5},{5,4},{6,7},{7,6},{8,9},{9,8},{10,11... | collective-permute-start | bytes 1769480 | tf_op jit(solution)/shard_map/term_two/ppermute | solution.py:39
  30.1 6.4 %collective-permute-start.12 = (bf16[4,9,32,256]{3,2,1,0:T(8,128)(2,1)S(1)}, bf16[4,9,32,256]{3,2,1,0:T(8,128)(2,1)S(1)}, u32[]{:S(2)}, u32[]{:S(2)}) collective-permute-start(bf16[4,9,32,256]{3,2,1,0:T(8,128)(2,1)S(1)} %get-tuple-element.35), channel_id=1, source_target_pairs={{0,1},{1,0},{2,3},{3,2},{4,5},{5,4},{6,7},{7,6},{8,9},{9,8},{10,11... | collective-permute-start | bytes 1769480 | tf_op jit(solution)/shard_map/term_one/ppermute | solution.py:39
  30.2 27.6 %collective-permute-start.11 = (bf16[2,544,256]{2,1,0:T(8,128)(2,1)S(1)}, bf16[2,544,256]{2,1,0:T(8,128)(2,1)S(1)}, u32[]{:S(2)}, u32[]{:S(2)}) collective-permute-start(bf16[2,544,256]{2,1,0:T(8,128)(2,1)S(1)} %get-tuple-element.34.message), channel_id=1, source_target_pairs={{8,0},{16,8},{24,16},{9,1},{17,9},{25,17},{10,2},{18,10},{26,18},{... | collective-permute-start | bytes 1671176 | tf_op jit(solution)/shard_map/late_back/ppermute | solution.py:46
  34.8 7.9 %collective-permute-start.16 = (bf16[2,9,32,256]{3,2,1,0:T(8,128)(2,1)S(1)}, bf16[2,9,32,256]{3,2,1,0:T(8,128)(2,1)S(1)}, u32[]{:S(2)}, u32[]{:S(2)}) collective-permute-start(bf16[2,9,32,256]{3,2,1,0:T(8,128)(2,1)S(1)} %get-tuple-element.44), channel_id=1, source_target_pairs={{0,2},{1,3},{2,0},{3,1},{4,6},{5,7},{6,4},{7,5},{8,10},{9,11},{10,... | collective-permute-start | bytes 884744 | tf_op jit(solution)/shard_map/term_two_near/ppermute | solution.py:39
  35.1 17.7 %copy-start.2 = (bf16[2,1,16,32,256]{4,3,2,1,0:T(8,128)(2,1)S(1)}, bf16[2,1,16,32,256]{4,3,2,1,0:T(8,128)(2,1)}, u32[]{:S(2)}) copy-start(bf16[2,1,16,32,256]{4,3,2,1,0:T(8,128)(2,1)} %fresh.3) | copy-start | bytes 1572868
  35.1 17.7 %collective-permute-start.10 = (bf16[544,256]{1,0:T(8,128)(2,1)S(1)}, bf16[544,256]{1,0:T(8,128)(2,1)S(1)}, u32[]{:S(2)}, u32[]{:S(2)}) collective-permute-start(bf16[544,256]{1,0:T(8,128)(2,1)S(1)} %get-tuple-element.32.own_second), channel_id=1, source_target_pairs={{0,8},{8,16},{16,24},{1,9},{9,17},{17,25},{2,10},{10,18},{18,26},{... | collective-permute-start | bytes 835592 | tf_op jit(solution)/shard_map/late_fwd/ppermute | solution.py:46
  37.2 17.7 %collective-permute-start.13 = (bf16[2,9,32,256]{3,2,1,0:T(8,128)(2,1)S(1)}, bf16[2,9,32,256]{3,2,1,0:T(8,128)(2,1)S(1)}, u32[]{:S(2)}, u32[]{:S(2)}) collective-permute-start(bf16[2,9,32,256]{3,2,1,0:T(8,128)(2,1)S(1)} %get-tuple-element.37), channel_id=1, source_target_pairs={{0,2},{1,3},{2,0},{3,1},{4,6},{5,7},{6,4},{7,5},{8,10},{9,11},{10,... | collective-permute-start | bytes 884744 | tf_op jit(solution)/shard_map/term_one_near/ppermute | solution.py:39
  43.3 12.3 %collective-permute-start.17 = (bf16[1,9,32,256]{3,2,1,0:T(8,128)(2,1)S(1)}, bf16[1,9,32,256]{3,2,1,0:T(8,128)(2,1)S(1)}, u32[]{:S(2)}, u32[]{:S(2)}) collective-permute-start(bf16[1,9,32,256]{3,2,1,0:T(8,128)(2,1)S(1)} %get-tuple-element.46), channel_id=1, source_target_pairs={{0,4},{1,5},{2,6},{3,7},{4,0},{5,1},{6,2},{7,3},{8,12},{9,13},{10,... | collective-permute-start | bytes 442376 | tf_op jit(solution)/shard_map/term_two_far/ppermute | solution.py:39
  55.5 9.8 %collective-permute-start.14 = (bf16[1,9,32,256]{3,2,1,0:T(8,128)(2,1)S(1)}, bf16[1,9,32,256]{3,2,1,0:T(8,128)(2,1)S(1)}, u32[]{:S(2)}, u32[]{:S(2)}) collective-permute-start(bf16[1,9,32,256]{3,2,1,0:T(8,128)(2,1)S(1)} %get-tuple-element.39), channel_id=1, source_target_pairs={{0,4},{1,5},{2,6},{3,7},{4,0},{5,1},{6,2},{7,3},{8,12},{9,13},{10,... | collective-permute-start | bytes 442376 | tf_op jit(solution)/shard_map/term_one_far/ppermute | solution.py:39
  56.2 9.1 %collective-permute-start.18 = (bf16[9,32,256]{2,1,0:T(8,128)(2,1)S(1)}, bf16[9,32,256]{2,1,0:T(8,128)(2,1)S(1)}, u32[]{:S(2)}, u32[]{:S(2)}) collective-permute-start(bf16[9,32,256]{2,1,0:T(8,128)(2,1)S(1)} %gather_sum_kernel.1), channel_id=1, source_target_pairs={{8,0},{16,8},{24,16},{9,1},{17,9},{25,17},{10,2},{18,10},{26,18},{... | collective-permute-start | bytes 442376 | tf_op jit(solution)/shard_map/below/ppermute | solution.py:46
where the time goes:
time: 66.8 us; the launch traced here: 66.6 us
  waiting for transfers between devices  24.9 us (37%)
  starting transfers between devices  21.2 us (32%)
  Pallas kernels  18.9 us (28%)
  between operations  0.83 us (1%)
    pallas_call x12, Pallas kernels, call(): pl.pallas_call(kernel, name=name, out_shape=out_shape, in_specs=[SMEM] +...  18.9 us
    ppermute x14, waiting for transfers between devices, swapped(): lax.ppermute(x, 'dp', [(i, i ^ bit) for i in range(lax.axis_size('dp'))])  13.7 us
    ppermute x5, waiting for transfers between devices, passed_along(): return lax.ppermute(block, 'segment', route)  11.3 us
    ppermute x14, starting transfers between devices, swapped(): lax.ppermute(x, 'dp', [(i, i ^ bit) for i in range(lax.axis_size('dp'))])  10.8 us
    ppermute x5, starting transfers between devices, passed_along(): return lax.ppermute(block, 'segment', route)  10.4 us
  transfers between devices with their start and end apart: 19, of which 6 were waited for; matrix products, arithmetic and copies ran while one was open for 1% of the time, Pallas kernels for 24%

commit v1 on v0

--- a/solution.py
+++ b/solution.py
@@ -12,12 +12,12 @@
 VMEM = pl.BlockSpec(memory_space=pltpu.VMEM)
 SMEM = pl.BlockSpec(memory_space=pltpu.SMEM)
 TAPS = 9
-PARITY, FIRST, LAST, PLACE = range(4)
+PARITY, FIRST, LAST, PLACE, ODD = range(5)
 X2, Y1, G2, X1, Y2, G1, FRESH, TOP, LINES = 0, 2, 4, 6, 7, 8, 9, 10, 11
 DIRECT = (2, 4, 8)
 STEP_TWO = 3
 COLLECT = 0
-GRAD_ONE = 3
+GRAD_ONE = 0
 
 
 def call(kernel, out_shape, operands, weight=0, scratch=(), limit=32):
@@ -39,11 +39,14 @@
         return lax.ppermute(x, "dp", [(i, i ^ bit) for i in range(lax.axis_size("dp"))])
 
 
+def moved(block, name, target):
+    devices = range(lax.axis_size("segment"))
+    with jax.named_scope(name):
+        return lax.ppermute(block, "segment", [(i, target(i)) for i in devices if target(i) in devices])
+
+
 def passed_along(block, distance, name):
-    devices = range(lax.axis_size("segment"))
-    route = [(i - distance, i) for i in devices if i - distance in devices]
-    with jax.named_scope(name):
-        return lax.ppermute(block, "segment", route)
+    return moved(block, name, lambda i: i + distance)
 
 
 def after(x, *others):
@@ -128,7 +131,7 @@
     return store_halves
 
 
-def collect_kernel(info, fwd_in, bwd_in, fresh, top_cot, lines, early_fwd, early_back):
+def collect_kernel(info, fwd_in, bwd_in, fresh, top_cot, lines, back, cross, around):
     parity = info[PARITY]
 
     def put(slot, tile, amount):
@@ -144,9 +147,10 @@
     put(G1, bwd_in.at[2, 0, 0], 1)
     put(FRESH, fresh.at[1, 0], 1)
     put(TOP, top_cot.at[1, 0], 1)
-    early_back[0] = bwd_in[0, 0, 0]
-    early_back[1] = bwd_in[3, 0, 0]
-    early_fwd[...] = fwd_in[1, 0, 0]
+    odd = info[ODD] == 1
+    back[...] = bwd_in[0, 0, 0]
+    cross[...] = jnp.where(odd, bwd_in[3, 0, 0], fwd_in[1, 0, 0])
+    around[...] = jnp.where(odd, fwd_in[1, 0, 0], bwd_in[3, 0, 0])
 
 
 def grad_one_kernel(info, lines, fwd_in, bwd_in, top_cot, *rest):
@@ -212,30 +216,31 @@
     grad_into(storing(info, outs, False), message[0, :amount], windows(ext, height, width))
 
 
-def forward_two_kernel(info, lines, early, second, fresh, weight, out, ext):
+def forward_two_kernel(info, lines, cross, around, second, fresh, weight, out, ext):
     height, width = fresh.shape[2:4]
     amount = height * width
-    shape = early.shape
+    shape = cross.shape
     first = info[FIRST] == 1
     stream = jnp.where(first, flat(fresh[1, 0]), second[:amount])
     near = jnp.where(first, lines[FRESH], second[amount:])
     unfold(ext, stream, near, None, info[PARITY], True)
     out[0, 0, 0] = stream.reshape(shape)
-    other = jnp.where(first, fresh[0, 0], early[...])
+    early = jnp.where(info[ODD] == 1, cross[...], around[...])
+    other = jnp.where(first, fresh[0, 0], early)
     branch = conv(windows(ext, height, width), weight).reshape(shape)
     out[1, 0, 0] = (other.astype(F32) + branch).astype(BF16)
 
 
-def backward_two_kernel(info, lines, early, message, own_second, fwd_in, top_cot, weight, out, ext):
+def backward_two_kernel(info, lines, back, cross, around, message, own_second, fwd_in, top_cot, weight, out, ext):
     height, width = top_cot.shape[2:4]
     amount = height * width
-    shape = early.shape[1:]
+    shape = back.shape
     last = info[LAST] == 1
     out_first = jnp.where(last, flat(fwd_in[1, 0, 0]), message[0, :amount])
     near = jnp.where(last, lines[X2], message[0, amount:])
     out[1, 0, 0] = out_first.reshape(shape)
     unfold(ext, out_first, near, None, info[PARITY], True)
-    out_second = jnp.where(last, own_second[:amount], flat(early[0])).reshape(shape)
+    out_second = jnp.where(last, own_second[:amount], flat(back[...])).reshape(shape)
     branch = conv(windows(ext, height, width), weight).reshape(shape)
     out[0, 0, 0] = (out_second.astype(F32) - branch).astype(BF16)
     cot_second = jnp.where(last, flat(top_cot[1, 0]), message[1, :amount])
@@ -243,7 +248,8 @@
     out[2, 0, 0] = cot_second.reshape(shape)
     unfold(ext, cot_second, near, None, info[PARITY], False)
     through = conv_transposed(windows(ext, height, width), weight).reshape(shape)
-    cot_first = jnp.where(last, top_cot[0, 0], early[1])
+    early = jnp.where(info[ODD] == 1, around[...], cross[...])
+    cot_first = jnp.where(last, top_cot[0, 0], early)
     kept = jnp.where(out[1, 0, 0].astype(F32) > 0, through, 0.0)
     out[3, 0, 0] = (cot_first.astype(F32) + kept).astype(BF16)
 
@@ -278,6 +284,7 @@
             (segment_pos == 0).astype(jnp.int32),
             (segment_pos == lax.axis_size("segment") - 1).astype(jnp.int32),
             dp_pos // 2,
+            segment_pos % 2,
         ]
     ).astype(jnp.int32)
     like = lambda x, dtype: jax.ShapeDtypeStruct(x.shape, dtype)
@@ -292,15 +299,16 @@
             mine.append(swapped(mine[k - low], 2 * low, "weight_z%d" % k))
 
     tile = lambda *lead: jax.ShapeDtypeStruct(lead + (height, width, channels), BF16)
-    lines, early_fwd, early_back = call(
+    lines, back, cross, around = call(
         collect_kernel,
-        (jax.ShapeDtypeStruct((LINES, width, channels), BF16), tile(), tile(2)),
+        (jax.ShapeDtypeStruct((LINES, width, channels), BF16), tile(), tile(), tile()),
         (info, fwd_in, bwd_in, fresh, top_cot),
         COLLECT * conv_flops,
         limit=60,
     )
     lines = swapped(lines, 1, "lines")
-    early_back = passed_along(early_back, -1, "early_back")
+    back = passed_along(back, -1, "back")
+    around = moved(around, "around_first", lambda i: i + 2 if i % 2 else i - 2)
 
     def grads(kernel, operands, weight):
         if not direct:
@@ -323,27 +331,31 @@
             stay, send = call(fold_kernel, (shape(F32), shape(BF16)), (after(info, *hold[1:]), stay, got))
         return stay[0], [swapped(send, bit, name + "_far")[0]]
 
-    terms_one = grads(grad_one_kernel, (info, lines, fwd_in, bwd_in, top_cot), GRAD_ONE * conv_flops)
+    terms_one = grads(grad_one_kernel, (after(info, back), lines, fwd_in, bwd_in, top_cot), GRAD_ONE * conv_flops)
     if direct:
         others = mine[:-1] + [after(mine[-1], terms_one[0])]
+        others[1] = after(others[1], mine[-1])
         pieces = mine + [swapped(x, 1, "weight_core%d" % k) for k, x in enumerate(others)]
-        early_fwd = after(early_fwd, pieces[-2])
+        cross = after(cross, pieces[-2])
     else:
         pieces = [lax.all_gather(shard, "dp", axis=1, tiled=True)]
 
-    early_fwd = passed_along(early_fwd, 1, "early_fwd")
+    cross = moved(cross, "cross", lambda i: i ^ 1)
 
     message, second, weight = call(
         step_one_kernel,
         (taller(2), taller(), jax.ShapeDtypeStruct((TAPS, channels, outs), BF16)),
-        (after(info, early_back), lines, fwd_in, bwd_in, *pieces),
+        (after(info, around, cross), lines, fwd_in, bwd_in, *pieces),
         1,
         [ext],
     )
     late_back = passed_along(message, -1, "late_back")
     late_fwd = passed_along(second, 1, "late_fwd")
-
-    terms_two = grads(functools.partial(grad_two_kernel, height, width), (after(info, early_fwd), message), 1)
+    last = lax.axis_size("segment") - 1
+    turn = lambda i: i ^ 1 if (i >= 2 if i % 2 else i <= last - 2) else -1
+    around = moved(after(around, message), "around_second", turn)
+
+    terms_two = grads(functools.partial(grad_two_kernel, height, width), (info, message), 1)
     own_one, parts_one = scattered("term_one", *terms_one)
     own_two, parts_two = scattered("term_two", *terms_two)
     below = call(gather_sum_kernel, like(shard, BF16), (info, own_two, *parts_two))
@@ -352,14 +364,14 @@
     fwd_out = call(
         forward_two_kernel,
         like(fwd_in, BF16),
-        (info, lines, early_fwd, late_fwd, fresh, weight),
+        (info, lines, cross, around, late_fwd, fresh, weight),
         STEP_TWO * conv_flops,
         [ext],
     )
     bwd_out = call(
         backward_two_kernel,
         like(bwd_in, BF16),
-        (info, lines, early_back, late_back, second, fwd_in, top_cot, weight),
+        (info, lines, back, cross, around, late_back, second, fwd_in, top_cot, weight),
         STEP_TWO * conv_flops,
         [ext],
     )

time: 66.8 us -> 65.7 us (0.984)
  the two profiles are of different devices: /device:TPU:7 before, /device:TPU:0 now
where the time goes in v1:
time: 65.7 us; the launch traced here: 65.4 us
  starting transfers between devices  29.2 us (44%)
  Pallas kernels  18 us (27%)
  waiting for transfers between devices  16.7 us (25%)
  between operations  0.84 us (1%)
  local copies, waits for them, and re-layouts  0.68 us (1%)
    pallas_call x12, Pallas kernels, call(): pl.pallas_call(kernel, name=name, out_shape=out_shape, in_specs=[SMEM] +...  18 us
    ppermute x7, starting transfers between devices, moved(): lax.ppermute(block, 'segment', [(i, target(i)) for i in devices if target...  16.6 us
    ppermute x14, starting transfers between devices, swapped(): lax.ppermute(x, 'dp', [(i, i ^ bit) for i in range(lax.axis_size('dp'))])  12.6 us
    ppermute x7, waiting for transfers between devices, moved(): lax.ppermute(block, 'segment', [(i, target(i)) for i in devices if target...  9.21 us
    ppermute x14, waiting for transfers between devices, swapped(): lax.ppermute(x, 'dp', [(i, i ^ bit) for i in range(lax.axis_size('dp'))])  7.46 us
  transfers between devices with their start and end apart: 21, of which 9 were waited for; matrix products, arithmetic and copies ran while one was open for 1% of the time, Pallas kernels for 19%

profile of v1, /device:TPU:0, one launch (start us, length us, event | category | flops | bytes accessed | tf_op | source)
XLA Modules:
  0.0 65.4 jit_solution(10315831565662689938)
XLA Ops:
  0.6 4.1 %collective-permute-start.1 = (bf16[9,32,256]{2,1,0:T(8,128)(2,1)}, bf16[9,32,256]{2,1,0:T(8,128)(2,1)S(1)}, u32[]{:S(2)}, u32[]{:S(2)}) collective-permute-start(bf16[9,32,256]{2,1,0:T(8,128)(2,1)} %bitcast.17), channel_id=1, source_target_pairs={{0,4},{1,5},{2,6},{3,7},{4,0},{5,1},{6,2},{7,3},{8,12},{9,13},{10,... | collective-permute-start | bytes 442376 | tf_op jit(solution)/shard_map/weight_z2/ppermute | solution.py:39
  4.7 0.7 %stack.31.info = s32[5]{0:T(128)} concatenate(s32[1]{0:T(128)} %bitcast, s32[1]{0:T(128)} %bitcast.1, s32[1]{0:T(128)} %bitcast.2, s32[1]{0:T(128)} %bitcast.3, s32[1]{0:T(128)} %bitcast.4), dimensions={0} | concatenate | bytes 40 | tf_op jit(solution)/shard_map/stack | solution.py:281
  5.4 0.0 copy-start
  5.4 0.0 copy-start.1
  5.4 0.0 copy-start.5
  5.4 2.8 %collect_kernel.1 = (bf16[11,32,256]{2,1,0:T(8,128)(2,1)}, bf16[16,32,256]{2,1,0:T(8,128)(2,1)}, bf16[16,32,256]{2,1,0:T(8,128)(2,1)}, bf16[16,32,256]{2,1,0:T(8,128)(2,1)}) custom-call(s32[5]{0:T(128)} %stack.31.info, bf16[2,1,1,16,32,256]{5,4,3,2,1,0:T(8,128)(2,1)} %fwd_in.7, bf16[4,1,1,16,32,256]{5,4,3,2,1,0:T(8,128)(2,1)} %bwd_in.5, ...), custom_call_target="tpu_custom_call" | custom-call | bytes 1 | tf_op jit(solution)/shard_map/collect_kernel/pallas_call | solution.py:25
  8.2 1.3 %collective-permute-start.9 = (bf16[16,32,256]{2,1,0:T(8,128)(2,1)}, bf16[16,32,256]{2,1,0:T(8,128)(2,1)S(1)}, u32[]{:S(2)}, u32[]{:S(2)}) collective-permute-start(bf16[16,32,256]{2,1,0:T(8,128)(2,1)} %get-tuple-element.34), channel_id=1, source_target_pairs={{8,0},{16,8},{24,16},{9,1},{17,9},{25,17},{10,2},{18,10},{26,18},{... | collective-permute-start | bytes 786440 | tf_op jit(solution)/shard_map/back/ppermute | solution.py:45
  9.5 2.5 %collective-permute-done.1.rest_2_ = bf16[9,32,256]{2,1,0:T(8,128)(2,1)S(1)} collective-permute-done((bf16[9,32,256]{2,1,0:T(8,128)(2,1)}, bf16[9,32,256]{2,1,0:T(8,128)(2,1)S(1)}, u32[]{:S(2)}, u32[]{:S(2)}) %collective-permute-start.1) | collective-permute-done | bytes 147488 | tf_op jit(solution)/shard_map/weight_z2/ppermute | solution.py:39
  12.0 0.0 collective-permute-start.2
  12.0 0.5 collective-permute-start
  12.5 0.0 copy-done.4
  12.5 0.8 %collective-permute-start.5 = (bf16[9,32,256]{2,1,0:T(8,128)(2,1)S(1)}, bf16[9,32,256]{2,1,0:T(8,128)(2,1)S(1)}, u32[]{:S(2)}, u32[]{:S(2)}) collective-permute-start(bf16[9,32,256]{2,1,0:T(8,128)(2,1)S(1)} %bitcast.18), channel_id=1, source_target_pairs={{0,2},{1,3},{2,0},{3,1},{4,6},{5,7},{6,4},{7,5},{8,10},{9,11},{10,... | collective-permute-start | bytes 442376 | tf_op jit(solution)/shard_map/weight_z1/ppermute | solution.py:39
  13.3 1.2 %collective-permute-start.6 = (bf16[9,32,256]{2,1,0:T(8,128)(2,1)S(1)}, bf16[9,32,256]{2,1,0:T(8,128)(2,1)S(1)}, u32[]{:S(2)}, u32[]{:S(2)}) collective-permute-start(bf16[9,32,256]{2,1,0:T(8,128)(2,1)S(1)} %collective-permute-done.1.rest_2_), channel_id=1, source_target_pairs={{0,2},{1,3},{2,0},{3,1},{4,6},{5,7},{6,4},{7,5},{8,10},{9,11},{10,... | collective-permute-start | bytes 442376 | tf_op jit(solution)/shard_map/weight_z3/ppermute | solution.py:39
  14.5 0.0 collective-permute-done.2.rest_6_
  14.5 1.3 %collective-permute-start.4 = (bf16[16,32,256]{2,1,0:T(8,128)(2,1)}, bf16[16,32,256]{2,1,0:T(8,128)(2,1)S(1)}, u32[]{:S(2)}, u32[]{:S(2)}) collective-permute-start(bf16[16,32,256]{2,1,0:T(8,128)(2,1)} %get-tuple-element.31), channel_id=1, source_target_pairs={{8,24},{16,0},{9,25},{17,1},{10,26},{18,2},{11,27},{19,3},{12,28},... | collective-permute-start | bytes 786440 | tf_op jit(solution)/shard_map/around_first/ppermute | solution.py:45
  15.8 2.3 %collective-permute-done.9.back = bf16[16,32,256]{2,1,0:T(8,128)(2,1)S(1)} collective-permute-done((bf16[16,32,256]{2,1,0:T(8,128)(2,1)}, bf16[16,32,256]{2,1,0:T(8,128)(2,1)S(1)}, u32[]{:S(2)}, u32[]{:S(2)}) %collective-permute-start.9) | collective-permute-done | bytes 262176 | tf_op jit(solution)/shard_map/back/ppermute | solution.py:45
  18.1 2.4 %collective-permute-start.3 = (bf16[16,32,256]{2,1,0:T(8,128)(2,1)}, bf16[16,32,256]{2,1,0:T(8,128)(2,1)S(1)}, u32[]{:S(2)}, u32[]{:S(2)}) collective-permute-start(bf16[16,32,256]{2,1,0:T(8,128)(2,1)} %get-tuple-element.30), channel_id=1, source_target_pairs={{0,8},{8,0},{16,24},{24,16},{1,9},{9,1},{17,25},{25,17},{2,10},{10... | collective-permute-start | bytes 786440 | tf_op jit(solution)/shard_map/cross/ppermute | solution.py:45
  20.5 0.0 collective-permute-done.lines
  20.5 0.0 collective-permute-start.7
  20.5 0.0 copy-done
  20.5 0.0 copy-done.1
  20.5 0.0 copy-done.2
  20.5 0.0 copy-done.5
  20.5 1.4 %grad_one_kernel.1 = (f32[4,9,32,256]{3,2,1,0:T(8,128)S(1)}, bf16[4,9,32,256]{3,2,1,0:T(8,128)(2,1)S(1)}) custom-call(s32[5]{0:T(128)S(1)} %copy-done.5, bf16[11,32,256]{2,1,0:T(8,128)(2,1)S(1)} %collective-permute-done.lines, bf16[2,1,1,16,32,256]{5,4,3,2,1,0:T(8,128)(2,1)S(1)} %copy-done.1, bf16[4,1,1,16,32,256]{5,4,3,2,1,0:T(8,128)(2,1)S(1)} %copy-done, ...), custom_call_target="tpu_custom_call" | custom-call | bytes 1 | tf_op jit(solution)/shard_map/grad_one_kernel/pallas_call | solution.py:25
  21.9 0.0 collective-permute-done.5.rest_1_
  22.0 0.0 collective-permute-done.6.rest_3_
  22.0 0.6 collective-permute-start.8
  22.5 0.1 collective-permute-start.10
  22.6 1.6 %collective-permute-done.4 = bf16[16,32,256]{2,1,0:T(8,128)(2,1)S(1)} collective-permute-done((bf16[16,32,256]{2,1,0:T(8,128)(2,1)}, bf16[16,32,256]{2,1,0:T(8,128)(2,1)S(1)}, u32[]{:S(2)}, u32[]{:S(2)}) %collective-permute-start.4) | collective-permute-done | bytes 262176 | tf_op jit(solution)/shard_map/around_first/ppermute | solution.py:45
  24.2 1.5 %collective-permute-done.3.cross = bf16[16,32,256]{2,1,0:T(8,128)(2,1)S(1)} collective-permute-done((bf16[16,32,256]{2,1,0:T(8,128)(2,1)}, bf16[16,32,256]{2,1,0:T(8,128)(2,1)S(1)}, u32[]{:S(2)}, u32[]{:S(2)}) %collective-permute-start.3) | collective-permute-done | bytes 262176 | tf_op jit(solution)/shard_map/cross/ppermute | solution.py:45
  25.8 0.0 collective-permute-done.7.rest_4_
  25.8 0.0 collective-permute-done.8.rest_5_
  25.8 0.0 collective-permute-done.10.rest_7_
  25.8 2.9 %step_one_kernel.1 = (bf16[2,544,256]{2,1,0:T(8,128)(2,1)S(1)}, bf16[544,256]{1,0:T(8,128)(2,1)S(1)}, bf16[9,256,256]{2,1,0:T(8,128)(2,1)S(1)}) custom-call(s32[5]{0:T(128)S(1)} %copy-done.5, bf16[11,32,256]{2,1,0:T(8,128)(2,1)S(1)} %collective-permute-done.lines, bf16[2,1,1,16,32,256]{5,4,3,2,1,0:T(8,128)(2,1)S(1)} %copy-done.1, ...), custom_call_target="tpu_custom_call" | custom-call | flops 1 | bytes 1 | tf_op jit(solution)/shard_map/step_one_kernel/pallas_call | solution.py:25
  28.7 1.4 %grad_two_kernel.1 = (f32[4,9,32,256]{3,2,1,0:T(8,128)S(1)}, bf16[4,9,32,256]{3,2,1,0:T(8,128)(2,1)S(1)}) custom-call(s32[5]{0:T(128)S(1)} %copy-done.5, bf16[2,544,256]{2,1,0:T(8,128)(2,1)S(1)} %get-tuple-element.38.message), custom_call_target="tpu_custom_call" | custom-call | flops 1 | bytes 1 | tf_op jit(solution)/shard_map/grad_two_kernel/pallas_call | solution.py:25
  30.1 0.1 collective-permute-start.17
  30.2 0.5 collective-permute-start.14
  30.7 1.3 %collective-permute-start.13 = (bf16[2,544,256]{2,1,0:T(8,128)(2,1)S(1)}, bf16[2,544,256]{2,1,0:T(8,128)(2,1)S(1)}, u32[]{:S(2)}, u32[]{:S(2)}) collective-permute-start(bf16[2,544,256]{2,1,0:T(8,128)(2,1)S(1)} %get-tuple-element.38.message), channel_id=1, source_target_pairs={{8,0},{16,8},{24,16},{9,1},{17,9},{25,17},{10,2},{18,10},{26,18},{... | collective-permute-start | bytes 1671176 | tf_op jit(solution)/shard_map/late_back/ppermute | solution.py:45
  32.0 0.2 collective-permute-done.17.got
  32.2 0.6 pair_sum_kernel.3
  32.8 1.6 %collective-permute-start.18 = (bf16[2,9,32,256]{3,2,1,0:T(8,128)(2,1)S(1)}, bf16[2,9,32,256]{3,2,1,0:T(8,128)(2,1)S(1)}, u32[]{:S(2)}, u32[]{:S(2)}) collective-permute-start(bf16[2,9,32,256]{3,2,1,0:T(8,128)(2,1)S(1)} %get-tuple-element.50), channel_id=1, source_target_pairs={{0,2},{1,3},{2,0},{3,1},{4,6},{5,7},{6,4},{7,5},{8,10},{9,11},{10,... | collective-permute-start | bytes 884744 | tf_op jit(solution)/shard_map/term_two_near/ppermute | solution.py:39
  34.5 4.5 %collective-permute-start.12 = (bf16[544,256]{1,0:T(8,128)(2,1)S(1)}, bf16[544,256]{1,0:T(8,128)(2,1)S(1)}, u32[]{:S(2)}, u32[]{:S(2)}) collective-permute-start(bf16[544,256]{1,0:T(8,128)(2,1)S(1)} %get-tuple-element.40.own_second), channel_id=1, source_target_pairs={{0,8},{8,16},{16,24},{1,9},{9,17},{17,25},{2,10},{10,18},{18,26},{... | collective-permute-start | bytes 835592 | tf_op jit(solution)/shard_map/late_fwd/ppermute | solution.py:45
  39.0 4.5 %collective-permute-start.11 = (bf16[16,32,256]{2,1,0:T(8,128)(2,1)S(1)}, bf16[16,32,256]{2,1,0:T(8,128)(2,1)S(1)}, u32[]{:S(2)}, u32[]{:S(2)}) collective-permute-start(bf16[16,32,256]{2,1,0:T(8,128)(2,1)S(1)} %collective-permute-done.4), channel_id=1, source_target_pairs={{0,8},{24,16},{1,9},{25,17},{2,10},{26,18},{3,11},{27,19},{4,12},{... | collective-permute-start | bytes 786440 | tf_op jit(solution)/shard_map/around_second/ppermute | solution.py:45
  43.5 0.0 collective-permute-done.14.got
  43.5 0.6 pair_sum_kernel.2
  44.2 0.5 collective-permute-start.15
  44.7 0.0 collective-permute-done.18.got
  44.7 0.6 fold_kernel.3
  45.3 2.0 %collective-permute-start.19 = (bf16[1,9,32,256]{3,2,1,0:T(8,128)(2,1)S(1)}, bf16[1,9,32,256]{3,2,1,0:T(8,128)(2,1)S(1)}, u32[]{:S(2)}, u32[]{:S(2)}) collective-permute-start(bf16[1,9,32,256]{3,2,1,0:T(8,128)(2,1)S(1)} %get-tuple-element.52), channel_id=1, source_target_pairs={{0,4},{1,5},{2,6},{3,7},{4,0},{5,1},{6,2},{7,3},{8,12},{9,13},{10,... | collective-permute-start | bytes 442376 | tf_op jit(solution)/shard_map/term_two_far/ppermute | solution.py:39
  47.3 2.8 %collective-permute-done.11.around = bf16[16,32,256]{2,1,0:T(8,128)(2,1)S(1)} collective-permute-done((bf16[16,32,256]{2,1,0:T(8,128)(2,1)S(1)}, bf16[16,32,256]{2,1,0:T(8,128)(2,1)S(1)}, u32[]{:S(2)}, u32[]{:S(2)}) %collective-permute-start.11) | collective-permute-done | bytes 262176 | tf_op jit(solution)/shard_map/around_second/ppermute | solution.py:45
  50.2 0.0 collective-permute-done.12.second
  50.2 0.0 copy-done.3
  50.2 2.2 %forward_two_kernel.1 = bf16[2,1,1,16,32,256]{5,4,3,2,1,0:T(8,128)(2,1)} custom-call(s32[5]{0:T(128)S(1)} %copy-done.5, bf16[11,32,256]{2,1,0:T(8,128)(2,1)S(1)} %collective-permute-done.lines, bf16[16,32,256]{2,1,0:T(8,128)(2,1)S(1)} %collective-permute-done.3.cross, bf16[16,32,256]{2,1,0:T(8,128)(2,1)S(1)} %collective-permute-done.11.around, ...), custom_call_target="tpu_custom_call" | custom-call | flops 1811939328 | bytes 1 | tf_op jit(solution)/shard_map/forward_two_kernel/pallas_call | solution.py:25
  52.3 3.0 %collective-permute-done.15.got = bf16[2,9,32,256]{3,2,1,0:T(8,128)(2,1)S(1)} collective-permute-done((bf16[2,9,32,256]{3,2,1,0:T(8,128)(2,1)S(1)}, bf16[2,9,32,256]{3,2,1,0:T(8,128)(2,1)S(1)}, u32[]{:S(2)}, u32[]{:S(2)}) %collective-permute-start.15) | collective-permute-done | bytes 294944 | tf_op jit(solution)/shard_map/term_one_near/ppermute | solution.py:39
  55.3 0.6 fold_kernel.2
  55.9 0.6 collective-permute-start.16
  56.5 0.0 collective-permute-done.19
  56.5 0.6 gather_sum_kernel.1
  57.0 1.3 %collective-permute-start.20 = (bf16[9,32,256]{2,1,0:T(8,128)(2,1)S(1)}, bf16[9,32,256]{2,1,0:T(8,128)(2,1)S(1)}, u32[]{:S(2)}, u32[]{:S(2)}) collective-permute-start(bf16[9,32,256]{2,1,0:T(8,128)(2,1)S(1)} %gather_sum_kernel.1), channel_id=1, source_target_pairs={{8,0},{16,8},{24,16},{9,1},{17,9},{25,17},{10,2},{18,10},{26,18},{... | collective-permute-start | bytes 442376 | tf_op jit(solution)/shard_map/below/ppermute | solution.py:45
  58.3 0.0 collective-permute-done.13.message
  58.4 3.0 %backward_two_kernel.1 = bf16[4,1,1,16,32,256]{5,4,3,2,1,0:T(8,128)(2,1)} custom-call(s32[5]{0:T(128)S(1)} %copy-done.5, bf16[11,32,256]{2,1,0:T(8,128)(2,1)S(1)} %collective-permute-done.lines, bf16[16,32,256]{2,1,0:T(8,128)(2,1)S(1)} %collective-permute-done.9.back, bf16[16,32,256]{2,1,0:T(8,128)(2,1)S(1)} %collective-permute-done.3.cross, ...), custom_call_target="tpu_custom_call" | custom-call | flops 1811939328 | bytes 1 | tf_op jit(solution)/shard_map/backward_two_kernel/pallas_call | solution.py:25
  61.3 1.8 %collective-permute-done.16 = bf16[1,9,32,256]{3,2,1,0:T(8,128)(2,1)S(1)} collective-permute-done((bf16[1,9,32,256]{3,2,1,0:T(8,128)(2,1)S(1)}, bf16[1,9,32,256]{3,2,1,0:T(8,128)(2,1)S(1)}, u32[]{:S(2)}, u32[]{:S(2)}) %collective-permute-start.16) | collective-permute-done | bytes 147488 | tf_op jit(solution)/shard_map/term_one_far/ppermute | solution.py:39
  63.1 0.9 %collective-permute-done.20.rest_1_ = bf16[9,32,256]{2,1,0:T(8,128)(2,1)S(1)} collective-permute-done((bf16[9,32,256]{2,1,0:T(8,128)(2,1)S(1)}, bf16[9,32,256]{2,1,0:T(8,128)(2,1)S(1)}, u32[]{:S(2)}, u32[]{:S(2)}) %collective-permute-start.20) | collective-permute-done | bytes 147488 | tf_op jit(solution)/shard_map/below/ppermute | solution.py:45
  64.1 1.3 %finish_kernel.1 = f32[9,32,256]{2,1,0:T(8,128)} custom-call(s32[5]{0:T(128)S(1)} %copy-done.5, f32[9,32,256]{2,1,0:T(8,128)S(1)} %bitcast.15, bf16[9,32,256]{2,1,0:T(8,128)(2,1)S(1)} %bitcast.21, bf16[9,32,256]{2,1,0:T(8,128)(2,1)S(1)} %collective-permute-done.20.rest_1_), custom_call_target="tpu_custom_call" | custom-call | bytes 1 | tf_op jit(solution)/shard_map/finish_kernel/pallas_call | solution.py:25
  (3 shorter events, 0.0 us)
Async XLA Ops:
  0.6 11.3 %collective-permute-start.1 = (bf16[9,32,256]{2,1,0:T(8,128)(2,1)}, bf16[9,32,256]{2,1,0:T(8,128)(2,1)S(1)}, u32[]{:S(2)}, u32[]{:S(2)}) collective-permute-start(bf16[9,32,256]{2,1,0:T(8,128)(2,1)} %bitcast.17), channel_id=1, source_target_pairs={{0,4},{1,5},{2,6},{3,7},{4,0},{5,1},{6,2},{7,3},{8,12},{9,13},{10,... | collective-permute-start | bytes 442376 | tf_op jit(solution)/shard_map/weight_z2/ppermute | solution.py:39
  5.4 7.1 %copy-start.4 = (bf16[1,32,9,256]{3,1,2,0:T(8,128)(2,1)S(1)}, bf16[1,32,9,256]{3,1,2,0:T(8,128)(2,1)}, u32[]{:S(2)}) copy-start(bf16[1,32,9,256]{3,1,2,0:T(8,128)(2,1)} %param.9) | copy-start | bytes 442372
  5.4 15.1 %copy-start = (bf16[4,1,1,16,32,256]{5,4,3,2,1,0:T(8,128)(2,1)S(1)}, bf16[4,1,1,16,32,256]{5,4,3,2,1,0:T(8,128)(2,1)}, u32[]{:S(2)}) copy-start(bf16[4,1,1,16,32,256]{5,4,3,2,1,0:T(8,128)(2,1)} %bwd_in.5) | copy-start | bytes 3145732
  5.4 15.1 %copy-start.1 = (bf16[2,1,1,16,32,256]{5,4,3,2,1,0:T(8,128)(2,1)S(1)}, bf16[2,1,1,16,32,256]{5,4,3,2,1,0:T(8,128)(2,1)}, u32[]{:S(2)}) copy-start(bf16[2,1,1,16,32,256]{5,4,3,2,1,0:T(8,128)(2,1)} %fwd_in.7) | copy-start | bytes 1572868
  5.4 15.1 %copy-start.2 = (bf16[2,1,16,32,256]{4,3,2,1,0:T(8,128)(2,1)S(1)}, bf16[2,1,16,32,256]{4,3,2,1,0:T(8,128)(2,1)}, u32[]{:S(2)}) copy-start(bf16[2,1,16,32,256]{4,3,2,1,0:T(8,128)(2,1)} %top_cot.5) | copy-start | bytes 1572868
  5.4 15.1 %copy-start.5 = (s32[5]{0:T(128)S(1)}, s32[5]{0:T(128)}, u32[]{:S(2)}) copy-start(s32[5]{0:T(128)} %stack.31.info) | copy-start | bytes 64
  8.2 9.9 %collective-permute-start.9 = (bf16[16,32,256]{2,1,0:T(8,128)(2,1)}, bf16[16,32,256]{2,1,0:T(8,128)(2,1)S(1)}, u32[]{:S(2)}, u32[]{:S(2)}) collective-permute-start(bf16[16,32,256]{2,1,0:T(8,128)(2,1)} %get-tuple-element.34), channel_id=1, source_target_pairs={{8,0},{16,8},{24,16},{9,1},{17,9},{25,17},{10,2},{18,10},{26,18},{... | collective-permute-start | bytes 786440 | tf_op jit(solution)/shard_map/back/ppermute | solution.py:45
  12.0 2.5 %collective-permute-start.2 = (bf16[9,32,256]{2,1,0:T(8,128)(2,1)S(1)}, bf16[9,32,256]{2,1,0:T(8,128)(2,1)S(1)}, u32[]{:S(2)}, u32[]{:S(2)}) collective-permute-start(bf16[9,32,256]{2,1,0:T(8,128)(2,1)S(1)} %collective-permute-done.1.rest_2_), channel_id=1, source_target_pairs={{0,1},{1,0},{2,3},{3,2},{4,5},{5,4},{6,7},{7,6},{8,9},{9,8},{10,11... | collective-permute-start | bytes 442376 | tf_op jit(solution)/shard_map/weight_core2/ppermute | solution.py:39
  12.0 8.5 %collective-permute-start = (bf16[11,32,256]{2,1,0:T(8,128)(2,1)}, bf16[11,32,256]{2,1,0:T(8,128)(2,1)S(1)}, u32[]{:S(2)}, u32[]{:S(2)}) collective-permute-start(bf16[11,32,256]{2,1,0:T(8,128)(2,1)} %get-tuple-element.28), channel_id=1, source_target_pairs={{0,1},{1,0},{2,3},{3,2},{4,5},{5,4},{6,7},{7,6},{8,9},{9,8},{10,11... | collective-permute-start | bytes 540680 | tf_op jit(solution)/shard_map/lines/ppermute | solution.py:39
  12.5 9.5 %collective-permute-start.5 = (bf16[9,32,256]{2,1,0:T(8,128)(2,1)S(1)}, bf16[9,32,256]{2,1,0:T(8,128)(2,1)S(1)}, u32[]{:S(2)}, u32[]{:S(2)}) collective-permute-start(bf16[9,32,256]{2,1,0:T(8,128)(2,1)S(1)} %bitcast.18), channel_id=1, source_target_pairs={{0,2},{1,3},{2,0},{3,1},{4,6},{5,7},{6,4},{7,5},{8,10},{9,11},{10,... | collective-permute-start | bytes 442376 | tf_op jit(solution)/shard_map/weight_z1/ppermute | solution.py:39
  13.3 8.7 %collective-permute-start.6 = (bf16[9,32,256]{2,1,0:T(8,128)(2,1)S(1)}, bf16[9,32,256]{2,1,0:T(8,128)(2,1)S(1)}, u32[]{:S(2)}, u32[]{:S(2)}) collective-permute-start(bf16[9,32,256]{2,1,0:T(8,128)(2,1)S(1)} %collective-permute-done.1.rest_2_), channel_id=1, source_target_pairs={{0,2},{1,3},{2,0},{3,1},{4,6},{5,7},{6,4},{7,5},{8,10},{9,11},{10,... | collective-permute-start | bytes 442376 | tf_op jit(solution)/shard_map/weight_z3/ppermute | solution.py:39
  14.5 9.7 %collective-permute-start.4 = (bf16[16,32,256]{2,1,0:T(8,128)(2,1)}, bf16[16,32,256]{2,1,0:T(8,128)(2,1)S(1)}, u32[]{:S(2)}, u32[]{:S(2)}) collective-permute-start(bf16[16,32,256]{2,1,0:T(8,128)(2,1)} %get-tuple-element.31), channel_id=1, source_target_pairs={{8,24},{16,0},{9,25},{17,1},{10,26},{18,2},{11,27},{19,3},{12,28},... | collective-permute-start | bytes 786440 | tf_op jit(solution)/shard_map/around_first/ppermute | solution.py:45
  18.1 7.7 %collective-permute-start.3 = (bf16[16,32,256]{2,1,0:T(8,128)(2,1)}, bf16[16,32,256]{2,1,0:T(8,128)(2,1)S(1)}, u32[]{:S(2)}, u32[]{:S(2)}) collective-permute-start(bf16[16,32,256]{2,1,0:T(8,128)(2,1)} %get-tuple-element.30), channel_id=1, source_target_pairs={{0,8},{8,0},{16,24},{24,16},{1,9},{9,1},{17,25},{25,17},{2,10},{10... | collective-permute-start | bytes 786440 | tf_op jit(solution)/shard_map/cross/ppermute | solution.py:45
  20.5 5.3 %collective-permute-start.7 = (bf16[9,32,256]{2,1,0:T(8,128)(2,1)S(1)}, bf16[9,32,256]{2,1,0:T(8,128)(2,1)S(1)}, u32[]{:S(2)}, u32[]{:S(2)}) collective-permute-start(bf16[9,32,256]{2,1,0:T(8,128)(2,1)S(1)} %bitcast.19), channel_id=1, source_target_pairs={{0,1},{1,0},{2,3},{3,2},{4,5},{5,4},{6,7},{7,6},{8,9},{9,8},{10,11... | collective-permute-start | bytes 442376 | tf_op jit(solution)/shard_map/weight_core0/ppermute | solution.py:39
  22.0 3.8 %collective-permute-start.8 = (bf16[9,32,256]{2,1,0:T(8,128)(2,1)S(1)}, bf16[9,32,256]{2,1,0:T(8,128)(2,1)S(1)}, u32[]{:S(2)}, u32[]{:S(2)}) collective-permute-start(bf16[9,32,256]{2,1,0:T(8,128)(2,1)S(1)} %collective-permute-done.5.rest_1_), channel_id=1, source_target_pairs={{0,1},{1,0},{2,3},{3,2},{4,5},{5,4},{6,7},{7,6},{8,9},{9,8},{10,11... | collective-permute-start | bytes 442376 | tf_op jit(solution)/shard_map/weight_core1/ppermute | solution.py:39
  22.5 3.3 %collective-permute-start.10 = (bf16[9,32,256]{2,1,0:T(8,128)(2,1)S(1)}, bf16[9,32,256]{2,1,0:T(8,128)(2,1)S(1)}, u32[]{:S(2)}, u32[]{:S(2)}) collective-permute-start(bf16[9,32,256]{2,1,0:T(8,128)(2,1)S(1)} %collective-permute-done.6.rest_3_), channel_id=1, source_target_pairs={{0,1},{1,0},{2,3},{3,2},{4,5},{5,4},{6,7},{7,6},{8,9},{9,8},{10,11... | collective-permute-start | bytes 442376 | tf_op jit(solution)/shard_map/weight_core3/ppermute | solution.py:39
  30.1 2.1 %collective-permute-start.17 = (bf16[4,9,32,256]{3,2,1,0:T(8,128)(2,1)S(1)}, bf16[4,9,32,256]{3,2,1,0:T(8,128)(2,1)S(1)}, u32[]{:S(2)}, u32[]{:S(2)}) collective-permute-start(bf16[4,9,32,256]{3,2,1,0:T(8,128)(2,1)S(1)} %get-tuple-element.48), channel_id=1, source_target_pairs={{0,1},{1,0},{2,3},{3,2},{4,5},{5,4},{6,7},{7,6},{8,9},{9,8},{10,11... | collective-permute-start | bytes 1769480 | tf_op jit(solution)/shard_map/term_two/ppermute | solution.py:39
  30.2 13.3 %collective-permute-start.14 = (bf16[4,9,32,256]{3,2,1,0:T(8,128)(2,1)S(1)}, bf16[4,9,32,256]{3,2,1,0:T(8,128)(2,1)S(1)}, u32[]{:S(2)}, u32[]{:S(2)}) collective-permute-start(bf16[4,9,32,256]{3,2,1,0:T(8,128)(2,1)S(1)} %get-tuple-element.42), channel_id=1, source_target_pairs={{0,1},{1,0},{2,3},{3,2},{4,5},{5,4},{6,7},{7,6},{8,9},{9,8},{10,11... | collective-permute-start | bytes 1769480 | tf_op jit(solution)/shard_map/term_one/ppermute | solution.py:39
  30.7 27.7 %collective-permute-start.13 = (bf16[2,544,256]{2,1,0:T(8,128)(2,1)S(1)}, bf16[2,544,256]{2,1,0:T(8,128)(2,1)S(1)}, u32[]{:S(2)}, u32[]{:S(2)}) collective-permute-start(bf16[2,544,256]{2,1,0:T(8,128)(2,1)S(1)} %get-tuple-element.38.message), channel_id=1, source_target_pairs={{8,0},{16,8},{24,16},{9,1},{17,9},{25,17},{10,2},{18,10},{26,18},{... | collective-permute-start | bytes 1671176 | tf_op jit(solution)/shard_map/late_back/ppermute | solution.py:45
  32.8 11.9 %collective-permute-start.18 = (bf16[2,9,32,256]{3,2,1,0:T(8,128)(2,1)S(1)}, bf16[2,9,32,256]{3,2,1,0:T(8,128)(2,1)S(1)}, u32[]{:S(2)}, u32[]{:S(2)}) collective-permute-start(bf16[2,9,32,256]{3,2,1,0:T(8,128)(2,1)S(1)} %get-tuple-element.50), channel_id=1, source_target_pairs={{0,2},{1,3},{2,0},{3,1},{4,6},{5,7},{6,4},{7,5},{8,10},{9,11},{10,... | collective-permute-start | bytes 884744 | tf_op jit(solution)/shard_map/term_two_near/ppermute | solution.py:39
  34.5 15.7 %copy-start.3 = (bf16[2,1,16,32,256]{4,3,2,1,0:T(8,128)(2,1)S(1)}, bf16[2,1,16,32,256]{4,3,2,1,0:T(8,128)(2,1)}, u32[]{:S(2)}) copy-start(bf16[2,1,16,32,256]{4,3,2,1,0:T(8,128)(2,1)} %fresh.3) | copy-start | bytes 1572868
  34.5 15.7 %collective-permute-start.12 = (bf16[544,256]{1,0:T(8,128)(2,1)S(1)}, bf16[544,256]{1,0:T(8,128)(2,1)S(1)}, u32[]{:S(2)}, u32[]{:S(2)}) collective-permute-start(bf16[544,256]{1,0:T(8,128)(2,1)S(1)} %get-tuple-element.40.own_second), channel_id=1, source_target_pairs={{0,8},{8,16},{16,24},{1,9},{9,17},{17,25},{2,10},{10,18},{18,26},{... | collective-permute-start | bytes 835592 | tf_op jit(solution)/shard_map/late_fwd/ppermute | solution.py:45
  39.0 11.2 %collective-permute-start.11 = (bf16[16,32,256]{2,1,0:T(8,128)(2,1)S(1)}, bf16[16,32,256]{2,1,0:T(8,128)(2,1)S(1)}, u32[]{:S(2)}, u32[]{:S(2)}) collective-permute-start(bf16[16,32,256]{2,1,0:T(8,128)(2,1)S(1)} %collective-permute-done.4), channel_id=1, source_target_pairs={{0,8},{24,16},{1,9},{25,17},{2,10},{26,18},{3,11},{27,19},{4,12},{... | collective-permute-start | bytes 786440 | tf_op jit(solution)/shard_map/around_second/ppermute | solution.py:45
  44.2 11.1 %collective-permute-start.15 = (bf16[2,9,32,256]{3,2,1,0:T(8,128)(2,1)S(1)}, bf16[2,9,32,256]{3,2,1,0:T(8,128)(2,1)S(1)}, u32[]{:S(2)}, u32[]{:S(2)}) collective-permute-start(bf16[2,9,32,256]{3,2,1,0:T(8,128)(2,1)S(1)} %get-tuple-element.44), channel_id=1, source_target_pairs={{0,2},{1,3},{2,0},{3,1},{4,6},{5,7},{6,4},{7,5},{8,10},{9,11},{10,... | collective-permute-start | bytes 884744 | tf_op jit(solution)/shard_map/term_one_near/ppermute | solution.py:39
  45.3 11.2 %collective-permute-start.19 = (bf16[1,9,32,256]{3,2,1,0:T(8,128)(2,1)S(1)}, bf16[1,9,32,256]{3,2,1,0:T(8,128)(2,1)S(1)}, u32[]{:S(2)}, u32[]{:S(2)}) collective-permute-start(bf16[1,9,32,256]{3,2,1,0:T(8,128)(2,1)S(1)} %get-tuple-element.52), channel_id=1, source_target_pairs={{0,4},{1,5},{2,6},{3,7},{4,0},{5,1},{6,2},{7,3},{8,12},{9,13},{10,... | collective-permute-start | bytes 442376 | tf_op jit(solution)/shard_map/term_two_far/ppermute | solution.py:39
  55.9 7.3 %collective-permute-start.16 = (bf16[1,9,32,256]{3,2,1,0:T(8,128)(2,1)S(1)}, bf16[1,9,32,256]{3,2,1,0:T(8,128)(2,1)S(1)}, u32[]{:S(2)}, u32[]{:S(2)}) collective-permute-start(bf16[1,9,32,256]{3,2,1,0:T(8,128)(2,1)S(1)} %get-tuple-element.46), channel_id=1, source_target_pairs={{0,4},{1,5},{2,6},{3,7},{4,0},{5,1},{6,2},{7,3},{8,12},{9,13},{10,... | collective-permute-start | bytes 442376 | tf_op jit(solution)/shard_map/term_one_far/ppermute | solution.py:39
  57.0 7.0 %collective-permute-start.20 = (bf16[9,32,256]{2,1,0:T(8,128)(2,1)S(1)}, bf16[9,32,256]{2,1,0:T(8,128)(2,1)S(1)}, u32[]{:S(2)}, u32[]{:S(2)}) collective-permute-start(bf16[9,32,256]{2,1,0:T(8,128)(2,1)S(1)} %gather_sum_kernel.1), channel_id=1, source_target_pairs={{8,0},{16,8},{24,16},{9,1},{17,9},{25,17},{10,2},{18,10},{26,18},{... | collective-permute-start | bytes 442376 | tf_op jit(solution)/shard_map/below/ppermute | solution.py:45

commit v2 on v1

--- a/solution.py
+++ b/solution.py
@@ -16,6 +16,7 @@
 X2, Y1, G2, X1, Y2, G1, FRESH, TOP, LINES = 0, 2, 4, 6, 7, 8, 9, 10, 11
 DIRECT = (2, 4, 8)
 STEP_TWO = 3
+STEP_ONE = 5
 COLLECT = 0
 GRAD_ONE = 0
 
@@ -306,6 +307,8 @@
         COLLECT * conv_flops,
         limit=60,
     )
+    if direct:
+        lines = after(lines, *mine[1:-1])
     lines = swapped(lines, 1, "lines")
     back = passed_along(back, -1, "back")
     around = moved(around, "around_first", lambda i: i + 2 if i % 2 else i - 2)
@@ -317,36 +320,37 @@
         shape = (jax.ShapeDtypeStruct(split, F32), jax.ShapeDtypeStruct(split, BF16))
         return call(kernel, shape, operands, weight, [ext])
 
-    def scattered(name, keep, give=None, hold=()):
+    def reduced(name, keep, give=None, hold=()):
         if not direct:
-            return lax.psum_scatter(keep, "dp", scatter_dimension=1, tiled=True), []
-        amount = places // 2
-        shape = lambda dtype: jax.ShapeDtypeStruct((amount,) + shard.shape, dtype)
-        got = swapped(give, 1, name)
-        stay, send = call(pair_sum_kernel, (shape(F32), shape(BF16)), (after(info, *hold[:1]), keep, got))
-        bit = 2
+            return lax.psum_scatter(keep, "dp", scatter_dimension=1, tiled=True), None
+        shape = lambda dtype: jax.ShapeDtypeStruct((places // 2,) + shard.shape, dtype)
+        return call(pair_sum_kernel, (shape(F32), shape(BF16)), (after(info, *hold), keep, swapped(give, 1, name)))
+
+    def scattered(name, stay, send, hold=()):
+        if not direct:
+            return stay, []
+        amount, bit = places // 2, 2
         while amount > 1:
             got = swapped(send, bit, name + "_near")
             amount, bit = amount // 2, 2 * bit
-            stay, send = call(fold_kernel, (shape(F32), shape(BF16)), (after(info, *hold[1:]), stay, got))
+            shape = lambda dtype: jax.ShapeDtypeStruct((amount,) + shard.shape, dtype)
+            stay, send = call(fold_kernel, (shape(F32), shape(BF16)), (after(info, *hold), stay, got))
         return stay[0], [swapped(send, bit, name + "_far")[0]]
 
     terms_one = grads(grad_one_kernel, (after(info, back), lines, fwd_in, bwd_in, top_cot), GRAD_ONE * conv_flops)
+    cross = moved(after(cross, lines), "cross", lambda i: i ^ 1)
+    sums_one = reduced("term_one", *terms_one, hold=(cross,))
     if direct:
         others = mine[:-1] + [after(mine[-1], terms_one[0])]
-        others[1] = after(others[1], mine[-1])
         pieces = mine + [swapped(x, 1, "weight_core%d" % k) for k, x in enumerate(others)]
-        cross = after(cross, pieces[-2])
     else:
         pieces = [lax.all_gather(shard, "dp", axis=1, tiled=True)]
-
-    cross = moved(cross, "cross", lambda i: i ^ 1)
 
     message, second, weight = call(
         step_one_kernel,
         (taller(2), taller(), jax.ShapeDtypeStruct((TAPS, channels, outs), BF16)),
-        (after(info, around, cross), lines, fwd_in, bwd_in, *pieces),
-        1,
+        (after(info, around), lines, fwd_in, bwd_in, *pieces),
+        STEP_ONE * conv_flops,
         [ext],
     )
     late_back = passed_along(message, -1, "late_back")
@@ -355,16 +359,17 @@
     turn = lambda i: i ^ 1 if (i >= 2 if i % 2 else i <= last - 2) else -1
     around = moved(after(around, message), "around_second", turn)
 
-    terms_two = grads(functools.partial(grad_two_kernel, height, width), (info, message), 1)
-    own_one, parts_one = scattered("term_one", *terms_one)
-    own_two, parts_two = scattered("term_two", *terms_two)
+    own_one, parts_one = scattered("term_one", *sums_one)
+    terms_two = grads(functools.partial(grad_two_kernel, height, width), (after(info, own_one), message), 1)
+    sums_two = reduced("term_two", *terms_two, hold=())
+    own_two, parts_two = scattered("term_two", *sums_two, hold=parts_one)
     below = call(gather_sum_kernel, like(shard, BF16), (info, own_two, *parts_two))
     from_above = passed_along(below, -1, "below")
 
     fwd_out = call(
         forward_two_kernel,
         like(fwd_in, BF16),
-        (info, lines, cross, around, late_fwd, fresh, weight),
+        (after(info, below), lines, cross, around, late_fwd, fresh, weight),
         STEP_TWO * conv_flops,
         [ext],
     )

time: 65.7 us -> 78.7 us (1.20)
  waiting for transfers between devices: 16.7 us -> 35.4 us
  starting transfers between devices: 29.2 us -> 23.5 us
    ppermute x14, waiting for transfers between devices: 7.46 us -> 21.6 us  [swapped(): lax.ppermute(x, 'dp', [(i, i ^ bit) for i in range(lax.axis_size('dp'))])]
    ppermute x7, waiting for transfers between devices: 9.21 us -> 13.8 us  [moved(): lax.ppermute(block, 'segment', [(i, target(i)) for i in devices if target...]
    ppermute x7, starting transfers between devices: 16.6 us -> 12.9 us  [moved(): lax.ppermute(block, 'segment', [(i, target(i)) for i in devices if target...]
    ppermute x14, starting transfers between devices: 12.6 us -> 10.5 us  [swapped(): lax.ppermute(x, 'dp', [(i, i ^ bit) for i in range(lax.axis_size('dp'))])]
  transfers between devices with their start and end apart: 21 -> 21, of which waited for: 9 -> 10; matrix products, arithmetic and copies ran while one was open for 1% -> 1% of each run, Pallas kernels for 19% -> 17%
where the time goes in v2:
time: 78.7 us; the launch traced here: 78.4 us
  waiting for transfers between devices  35.4 us (45%)
  starting transfers between devices  23.5 us (30%)
  Pallas kernels  18 us (23%)
  between operations  0.89 us (1%)
    ppermute x14, waiting for transfers between devices, swapped(): lax.ppermute(x, 'dp', [(i, i ^ bit) for i in range(lax.axis_size('dp'))])  21.6 us
    pallas_call x12, Pallas kernels, call(): pl.pallas_call(kernel, name=name, out_shape=out_shape, in_specs=[SMEM] +...  18 us
    ppermute x7, waiting for transfers between devices, moved(): lax.ppermute(block, 'segment', [(i, target(i)) for i in devices if target...  13.8 us
    ppermute x7, starting transfers between devices, moved(): lax.ppermute(block, 'segment', [(i, target(i)) for i in devices if target...  12.9 us
    ppermute x14, starting transfers between devices, swapped(): lax.ppermute(x, 'dp', [(i, i ^ bit) for i in range(lax.axis_size('dp'))])  10.5 us
  transfers between devices with their start and end apart: 21, of which 10 were waited for; matrix products, arithmetic and copies ran while one was open for 1% of the time, Pallas kernels for 17%

profile of v2, /device:TPU:0, one launch (start us, length us, event | category | flops | bytes accessed | tf_op | source)
XLA Modules:
  0.0 78.4 jit_solution(4228143619014559961)
XLA Ops:
  0.6 3.1 %collective-permute-start = (bf16[9,32,256]{2,1,0:T(8,128)(2,1)}, bf16[9,32,256]{2,1,0:T(8,128)(2,1)S(1)}, u32[]{:S(2)}, u32[]{:S(2)}) collective-permute-start(bf16[9,32,256]{2,1,0:T(8,128)(2,1)} %bitcast.19), channel_id=1, source_target_pairs={{0,2},{1,3},{2,0},{3,1},{4,6},{5,7},{6,4},{7,5},{8,10},{9,11},{10,... | collective-permute-start | bytes 442376 | tf_op jit(solution)/shard_map/weight_z1/ppermute | solution.py:40
  3.7 2.6 %collective-permute-start.1 = (bf16[9,32,256]{2,1,0:T(8,128)(2,1)}, bf16[9,32,256]{2,1,0:T(8,128)(2,1)S(1)}, u32[]{:S(2)}, u32[]{:S(2)}) collective-permute-start(bf16[9,32,256]{2,1,0:T(8,128)(2,1)} %bitcast.20), channel_id=1, source_target_pairs={{0,4},{1,5},{2,6},{3,7},{4,0},{5,1},{6,2},{7,3},{8,12},{9,13},{10,... | collective-permute-start | bytes 442376 | tf_op jit(solution)/shard_map/weight_z2/ppermute | solution.py:40
  6.3 0.7 stack.31.info
  7.0 2.8 %collect_kernel.1 = (bf16[11,32,256]{2,1,0:T(8,128)(2,1)}, bf16[16,32,256]{2,1,0:T(8,128)(2,1)}, bf16[16,32,256]{2,1,0:T(8,128)(2,1)}, bf16[16,32,256]{2,1,0:T(8,128)(2,1)}) custom-call(s32[5]{0:T(128)} %stack.31.info, bf16[2,1,1,16,32,256]{5,4,3,2,1,0:T(8,128)(2,1)} %fwd_in.7, bf16[4,1,1,16,32,256]{5,4,3,2,1,0:T(8,128)(2,1)} %bwd_in.5, ...), custom_call_target="tpu_custom_call" | custom-call | bytes 1 | tf_op jit(solution)/shard_map/collect_kernel/pallas_call | solution.py:26
  9.8 1.4 %collective-permute-start.4 = (bf16[16,32,256]{2,1,0:T(8,128)(2,1)}, bf16[16,32,256]{2,1,0:T(8,128)(2,1)S(1)}, u32[]{:S(2)}, u32[]{:S(2)}) collective-permute-start(bf16[16,32,256]{2,1,0:T(8,128)(2,1)} %get-tuple-element.37), channel_id=1, source_target_pairs={{8,0},{16,8},{24,16},{9,1},{17,9},{25,17},{10,2},{18,10},{26,18},{... | collective-permute-start | bytes 786440 | tf_op jit(solution)/shard_map/back/ppermute | solution.py:46
  11.2 0.0 collective-permute-done.rest_1_
  11.2 2.1 %collective-permute-done.1.rest_2_ = bf16[9,32,256]{2,1,0:T(8,128)(2,1)S(1)} collective-permute-done((bf16[9,32,256]{2,1,0:T(8,128)(2,1)}, bf16[9,32,256]{2,1,0:T(8,128)(2,1)S(1)}, u32[]{:S(2)}, u32[]{:S(2)}) %collective-permute-start.1) | collective-permute-done | bytes 147488 | tf_op jit(solution)/shard_map/weight_z2/ppermute | solution.py:40
  13.4 0.0 collective-permute-start.2
  13.4 6.1 %collective-permute-done.4.back = bf16[16,32,256]{2,1,0:T(8,128)(2,1)S(1)} collective-permute-done((bf16[16,32,256]{2,1,0:T(8,128)(2,1)}, bf16[16,32,256]{2,1,0:T(8,128)(2,1)S(1)}, u32[]{:S(2)}, u32[]{:S(2)}) %collective-permute-start.4) | collective-permute-done | bytes 262176 | tf_op jit(solution)/shard_map/back/ppermute | solution.py:46
  19.5 0.0 collective-permute-done.2.lines
  19.5 0.0 copy-done
  19.5 0.0 copy-done.1
  19.5 0.0 copy-done.2
  19.5 0.0 copy-done.4
  19.5 1.4 %grad_one_kernel.1 = (f32[4,9,32,256]{3,2,1,0:T(8,128)S(1)}, bf16[4,9,32,256]{3,2,1,0:T(8,128)(2,1)S(1)}) custom-call(s32[5]{0:T(128)S(1)} %copy-done.4, bf16[11,32,256]{2,1,0:T(8,128)(2,1)S(1)} %collective-permute-done.2.lines, bf16[2,1,1,16,32,256]{5,4,3,2,1,0:T(8,128)(2,1)S(1)} %copy-done.1, bf16[4,1,1,16,32,256]{5,4,3,2,1,0:T(8,128)(2,1)S(1)} %copy-done, ...), custom_call_target="tpu_custom_call" | custom-call | bytes 1 | tf_op jit(solution)/shard_map/grad_one_kernel/pallas_call | solution.py:26
  21.0 0.1 collective-permute-start.5
  21.1 0.0 copy-done.7
  21.1 2.5 %collective-permute-start.3 = (bf16[16,32,256]{2,1,0:T(8,128)(2,1)S(1)}, bf16[16,32,256]{2,1,0:T(8,128)(2,1)S(1)}, u32[]{:S(2)}, u32[]{:S(2)}) collective-permute-start(bf16[16,32,256]{2,1,0:T(8,128)(2,1)S(1)} %copy-done.7), channel_id=1, source_target_pairs={{0,8},{8,0},{16,24},{24,16},{1,9},{9,1},{17,25},{25,17},{2,10},{10... | collective-permute-start | bytes 786440 | tf_op jit(solution)/shard_map/cross/ppermute | solution.py:46
  23.5 0.4 collective-permute-start.9
  24.0 0.0 copy-done.6
  24.0 1.3 %collective-permute-start.8 = (bf16[16,32,256]{2,1,0:T(8,128)(2,1)S(1)}, bf16[16,32,256]{2,1,0:T(8,128)(2,1)S(1)}, u32[]{:S(2)}, u32[]{:S(2)}) collective-permute-start(bf16[16,32,256]{2,1,0:T(8,128)(2,1)S(1)} %copy-done.6), channel_id=1, source_target_pairs={{8,24},{16,0},{9,25},{17,1},{10,26},{18,2},{11,27},{19,3},{12,28},... | collective-permute-start | bytes 786440 | tf_op jit(solution)/shard_map/around_first/ppermute | solution.py:46
  25.3 0.0 copy-done.5
  25.3 0.1 collective-permute-start.10
  25.4 4.1 %collective-permute-done.9.rest_3_ = bf16[9,32,256]{2,1,0:T(8,128)(2,1)S(1)} collective-permute-done((bf16[9,32,256]{2,1,0:T(8,128)(2,1)S(1)}, bf16[9,32,256]{2,1,0:T(8,128)(2,1)S(1)}, u32[]{:S(2)}, u32[]{:S(2)}) %collective-permute-start.9) | collective-permute-done | bytes 147488 | tf_op jit(solution)/shard_map/weight_z3/ppermute | solution.py:40
  29.4 0.0 collective-permute-start.11
  29.4 1.0 %collective-permute-done.3.cross = bf16[16,32,256]{2,1,0:T(8,128)(2,1)S(1)} collective-permute-done((bf16[16,32,256]{2,1,0:T(8,128)(2,1)S(1)}, bf16[16,32,256]{2,1,0:T(8,128)(2,1)S(1)}, u32[]{:S(2)}, u32[]{:S(2)}) %collective-permute-start.3) | collective-permute-done | bytes 262176 | tf_op jit(solution)/shard_map/cross/ppermute | solution.py:46
  30.4 0.0 collective-permute-start.12
  30.4 0.0 collective-permute-done.5.got
  30.4 0.5 collective-permute-start.13
  30.9 0.6 pair_sum_kernel.2
  31.6 2.4 %collective-permute-done.8 = bf16[16,32,256]{2,1,0:T(8,128)(2,1)S(1)} collective-permute-done((bf16[16,32,256]{2,1,0:T(8,128)(2,1)S(1)}, bf16[16,32,256]{2,1,0:T(8,128)(2,1)S(1)}, u32[]{:S(2)}, u32[]{:S(2)}) %collective-permute-start.8) | collective-permute-done | bytes 262176 | tf_op jit(solution)/shard_map/around_first/ppermute | solution.py:46
  34.0 1.6 %collective-permute-start.6 = (bf16[2,9,32,256]{3,2,1,0:T(8,128)(2,1)S(1)}, bf16[2,9,32,256]{3,2,1,0:T(8,128)(2,1)S(1)}, u32[]{:S(2)}, u32[]{:S(2)}) collective-permute-start(bf16[2,9,32,256]{3,2,1,0:T(8,128)(2,1)S(1)} %get-tuple-element.42), channel_id=1, source_target_pairs={{0,2},{1,3},{2,0},{3,1},{4,6},{5,7},{6,4},{7,5},{8,10},{9,11},{10,... | collective-permute-start | bytes 884744 | tf_op jit(solution)/shard_map/term_one_near/ppermute | solution.py:40
  35.5 0.0 collective-permute-done.10.rest_4_
  35.5 0.0 collective-permute-done.11.rest_5_
  35.5 0.0 collective-permute-done.12.rest_6_
  35.5 0.0 collective-permute-done.13.rest_7_
  35.6 2.9 %step_one_kernel.1 = (bf16[2,544,256]{2,1,0:T(8,128)(2,1)S(1)}, bf16[544,256]{1,0:T(8,128)(2,1)S(1)}, bf16[9,256,256]{2,1,0:T(8,128)(2,1)S(1)}) custom-call(s32[5]{0:T(128)S(1)} %copy-done.4, bf16[11,32,256]{2,1,0:T(8,128)(2,1)S(1)} %collective-permute-done.2.lines, bf16[2,1,1,16,32,256]{5,4,3,2,1,0:T(8,128)(2,1)S(1)} %copy-done.1, ...), custom_call_target="tpu_custom_call" | custom-call | flops 3019898880 | bytes 1 | tf_op jit(solution)/shard_map/step_one_kernel/pallas_call | solution.py:26
  38.4 3.4 %collective-permute-done.6.got = bf16[2,9,32,256]{3,2,1,0:T(8,128)(2,1)S(1)} collective-permute-done((bf16[2,9,32,256]{3,2,1,0:T(8,128)(2,1)S(1)}, bf16[2,9,32,256]{3,2,1,0:T(8,128)(2,1)S(1)}, u32[]{:S(2)}, u32[]{:S(2)}) %collective-permute-start.6) | collective-permute-done | bytes 294944 | tf_op jit(solution)/shard_map/term_one_near/ppermute | solution.py:40
  41.9 0.6 fold_kernel.2
  42.5 1.4 %grad_two_kernel.1 = (f32[4,9,32,256]{3,2,1,0:T(8,128)S(1)}, bf16[4,9,32,256]{3,2,1,0:T(8,128)(2,1)S(1)}) custom-call(s32[5]{0:T(128)S(1)} %copy-done.4, bf16[2,544,256]{2,1,0:T(8,128)(2,1)S(1)} %get-tuple-element.50.message), custom_call_target="tpu_custom_call" | custom-call | flops 1 | bytes 1 | tf_op jit(solution)/shard_map/grad_two_kernel/pallas_call | solution.py:26
  43.9 0.1 collective-permute-start.14
  44.0 1.3 %collective-permute-start.19 = (bf16[2,544,256]{2,1,0:T(8,128)(2,1)S(1)}, bf16[2,544,256]{2,1,0:T(8,128)(2,1)S(1)}, u32[]{:S(2)}, u32[]{:S(2)}) collective-permute-start(bf16[2,544,256]{2,1,0:T(8,128)(2,1)S(1)} %get-tuple-element.50.message), channel_id=1, source_target_pairs={{8,0},{16,8},{24,16},{9,1},{17,9},{25,17},{10,2},{18,10},{26,18},{... | collective-permute-start | bytes 1671176 | tf_op jit(solution)/shard_map/late_back/ppermute | solution.py:46
  45.3 0.7 collective-permute-done.14.got
  46.0 0.6 pair_sum_kernel.3
  46.6 1.6 %collective-permute-start.15 = (bf16[2,9,32,256]{3,2,1,0:T(8,128)(2,1)S(1)}, bf16[2,9,32,256]{3,2,1,0:T(8,128)(2,1)S(1)}, u32[]{:S(2)}, u32[]{:S(2)}) collective-permute-start(bf16[2,9,32,256]{3,2,1,0:T(8,128)(2,1)S(1)} %get-tuple-element.54), channel_id=1, source_target_pairs={{0,2},{1,3},{2,0},{3,1},{4,6},{5,7},{6,4},{7,5},{8,10},{9,11},{10,... | collective-permute-start | bytes 884744 | tf_op jit(solution)/shard_map/term_two_near/ppermute | solution.py:40
  48.3 3.9 %collective-permute-start.17 = (bf16[16,32,256]{2,1,0:T(8,128)(2,1)S(1)}, bf16[16,32,256]{2,1,0:T(8,128)(2,1)S(1)}, u32[]{:S(2)}, u32[]{:S(2)}) collective-permute-start(bf16[16,32,256]{2,1,0:T(8,128)(2,1)S(1)} %collective-permute-done.8), channel_id=1, source_target_pairs={{0,8},{24,16},{1,9},{25,17},{2,10},{26,18},{3,11},{27,19},{4,12},{... | collective-permute-start | bytes 786440 | tf_op jit(solution)/shard_map/around_second/ppermute | solution.py:46
  52.2 0.4 collective-permute-start.7
  52.6 1.3 %collective-permute-start.18 = (bf16[544,256]{1,0:T(8,128)(2,1)S(1)}, bf16[544,256]{1,0:T(8,128)(2,1)S(1)}, u32[]{:S(2)}, u32[]{:S(2)}) collective-permute-start(bf16[544,256]{1,0:T(8,128)(2,1)S(1)} %get-tuple-element.59.own_second), channel_id=1, source_target_pairs={{0,8},{8,16},{16,24},{1,9},{9,17},{17,25},{2,10},{10,18},{18,26},{... | collective-permute-start | bytes 835592 | tf_op jit(solution)/shard_map/late_fwd/ppermute | solution.py:46
  53.9 7.8 %collective-permute-done.7 = bf16[1,9,32,256]{3,2,1,0:T(8,128)(2,1)S(1)} collective-permute-done((bf16[1,9,32,256]{3,2,1,0:T(8,128)(2,1)S(1)}, bf16[1,9,32,256]{3,2,1,0:T(8,128)(2,1)S(1)}, u32[]{:S(2)}, u32[]{:S(2)}) %collective-permute-start.7) | collective-permute-done | bytes 147488 | tf_op jit(solution)/shard_map/term_one_far/ppermute | solution.py:40
  61.7 0.0 collective-permute-done.15.got
  61.7 0.6 fold_kernel.3
  62.3 0.1 collective-permute-start.16
  62.3 0.0 collective-permute-done.17.around
  62.3 0.0 collective-permute-done.19.message
  62.4 0.0 copy-start.3
  62.4 3.0 %backward_two_kernel.1 = bf16[4,1,1,16,32,256]{5,4,3,2,1,0:T(8,128)(2,1)} custom-call(s32[5]{0:T(128)S(1)} %copy-done.4, bf16[11,32,256]{2,1,0:T(8,128)(2,1)S(1)} %collective-permute-done.2.lines, bf16[16,32,256]{2,1,0:T(8,128)(2,1)S(1)} %collective-permute-done.4.back, bf16[16,32,256]{2,1,0:T(8,128)(2,1)S(1)} %collective-permute-done.3.cross, ...), custom_call_target="tpu_custom_call" | custom-call | flops 1811939328 | bytes 1 | tf_op jit(solution)/shard_map/backward_two_kernel/pallas_call | solution.py:26
  65.3 3.5 %collective-permute-done.16 = bf16[1,9,32,256]{3,2,1,0:T(8,128)(2,1)S(1)} collective-permute-done((bf16[1,9,32,256]{3,2,1,0:T(8,128)(2,1)S(1)}, bf16[1,9,32,256]{3,2,1,0:T(8,128)(2,1)S(1)}, u32[]{:S(2)}, u32[]{:S(2)}) %collective-permute-start.16) | collective-permute-done | bytes 147488 | tf_op jit(solution)/shard_map/term_two_far/ppermute | solution.py:40
  68.8 0.6 gather_sum_kernel.1
  69.4 1.3 %collective-permute-start.20 = (bf16[9,32,256]{2,1,0:T(8,128)(2,1)S(1)}, bf16[9,32,256]{2,1,0:T(8,128)(2,1)S(1)}, u32[]{:S(2)}, u32[]{:S(2)}) collective-permute-start(bf16[9,32,256]{2,1,0:T(8,128)(2,1)S(1)} %gather_sum_kernel.1), channel_id=1, source_target_pairs={{8,0},{16,8},{24,16},{9,1},{17,9},{25,17},{10,2},{18,10},{26,18},{... | collective-permute-start | bytes 442376 | tf_op jit(solution)/shard_map/below/ppermute | solution.py:46
  70.7 0.0 collective-permute-done.18.second
  70.7 0.0 copy-done.3
  70.7 2.2 %forward_two_kernel.1 = bf16[2,1,1,16,32,256]{5,4,3,2,1,0:T(8,128)(2,1)} custom-call(s32[5]{0:T(128)S(1)} %copy-done.4, bf16[11,32,256]{2,1,0:T(8,128)(2,1)S(1)} %collective-permute-done.2.lines, bf16[16,32,256]{2,1,0:T(8,128)(2,1)S(1)} %collective-permute-done.3.cross, bf16[16,32,256]{2,1,0:T(8,128)(2,1)S(1)} %collective-permute-done.17.around, ...), custom_call_target="tpu_custom_call" | custom-call | flops 1811939328 | bytes 1 | tf_op jit(solution)/shard_map/forward_two_kernel/pallas_call | solution.py:26
  72.9 4.3 %collective-permute-done.20.rest_1_ = bf16[9,32,256]{2,1,0:T(8,128)(2,1)S(1)} collective-permute-done((bf16[9,32,256]{2,1,0:T(8,128)(2,1)S(1)}, bf16[9,32,256]{2,1,0:T(8,128)(2,1)S(1)}, u32[]{:S(2)}, u32[]{:S(2)}) %collective-permute-start.20) | collective-permute-done | bytes 147488 | tf_op jit(solution)/shard_map/below/ppermute | solution.py:46
  77.1 1.3 %finish_kernel.1 = f32[9,32,256]{2,1,0:T(8,128)} custom-call(s32[5]{0:T(128)S(1)} %copy-done.4, f32[9,32,256]{2,1,0:T(8,128)S(1)} %bitcast.15, bf16[9,32,256]{2,1,0:T(8,128)(2,1)S(1)} %bitcast.17, bf16[9,32,256]{2,1,0:T(8,128)(2,1)S(1)} %collective-permute-done.20.rest_1_), custom_call_target="tpu_custom_call" | custom-call | bytes 1 | tf_op jit(solution)/shard_map/finish_kernel/pallas_call | solution.py:26
  (7 shorter events, 0.0 us)
Async XLA Ops:
  0.6 10.6 %collective-permute-start = (bf16[9,32,256]{2,1,0:T(8,128)(2,1)}, bf16[9,32,256]{2,1,0:T(8,128)(2,1)S(1)}, u32[]{:S(2)}, u32[]{:S(2)}) collective-permute-start(bf16[9,32,256]{2,1,0:T(8,128)(2,1)} %bitcast.19), channel_id=1, source_target_pairs={{0,2},{1,3},{2,0},{3,1},{4,6},{5,7},{6,4},{7,5},{8,10},{9,11},{10,... | collective-permute-start | bytes 442376 | tf_op jit(solution)/shard_map/weight_z1/ppermute | solution.py:40
  3.7 9.6 %collective-permute-start.1 = (bf16[9,32,256]{2,1,0:T(8,128)(2,1)}, bf16[9,32,256]{2,1,0:T(8,128)(2,1)S(1)}, u32[]{:S(2)}, u32[]{:S(2)}) collective-permute-start(bf16[9,32,256]{2,1,0:T(8,128)(2,1)} %bitcast.20), channel_id=1, source_target_pairs={{0,4},{1,5},{2,6},{3,7},{4,0},{5,1},{6,2},{7,3},{8,12},{9,13},{10,... | collective-permute-start | bytes 442376 | tf_op jit(solution)/shard_map/weight_z2/ppermute | solution.py:40
  7.0 12.5 %copy-start = (bf16[4,1,1,16,32,256]{5,4,3,2,1,0:T(8,128)(2,1)S(1)}, bf16[4,1,1,16,32,256]{5,4,3,2,1,0:T(8,128)(2,1)}, u32[]{:S(2)}) copy-start(bf16[4,1,1,16,32,256]{5,4,3,2,1,0:T(8,128)(2,1)} %bwd_in.5) | copy-start | bytes 3145732
  7.0 12.5 %copy-start.1 = (bf16[2,1,1,16,32,256]{5,4,3,2,1,0:T(8,128)(2,1)S(1)}, bf16[2,1,1,16,32,256]{5,4,3,2,1,0:T(8,128)(2,1)}, u32[]{:S(2)}) copy-start(bf16[2,1,1,16,32,256]{5,4,3,2,1,0:T(8,128)(2,1)} %fwd_in.7) | copy-start | bytes 1572868
  7.0 12.5 %copy-start.2 = (bf16[2,1,16,32,256]{4,3,2,1,0:T(8,128)(2,1)S(1)}, bf16[2,1,16,32,256]{4,3,2,1,0:T(8,128)(2,1)}, u32[]{:S(2)}) copy-start(bf16[2,1,16,32,256]{4,3,2,1,0:T(8,128)(2,1)} %top_cot.5) | copy-start | bytes 1572868
  7.0 12.5 %copy-start.4 = (s32[5]{0:T(128)S(1)}, s32[5]{0:T(128)}, u32[]{:S(2)}) copy-start(s32[5]{0:T(128)} %stack.31.info) | copy-start | bytes 64
  9.8 11.3 %copy-start.7 = (bf16[16,32,256]{2,1,0:T(8,128)(2,1)S(1)}, bf16[16,32,256]{2,1,0:T(8,128)(2,1)}, u32[]{:S(2)}) copy-start(bf16[16,32,256]{2,1,0:T(8,128)(2,1)} %get-tuple-element.35) | copy-start | bytes 786436
  9.8 14.2 %copy-start.6 = (bf16[16,32,256]{2,1,0:T(8,128)(2,1)S(1)}, bf16[16,32,256]{2,1,0:T(8,128)(2,1)}, u32[]{:S(2)}) copy-start(bf16[16,32,256]{2,1,0:T(8,128)(2,1)} %get-tuple-element.47) | copy-start | bytes 786436
  9.8 15.5 %copy-start.5 = (bf16[1,32,9,256]{3,1,2,0:T(8,128)(2,1)S(1)}, bf16[1,32,9,256]{3,1,2,0:T(8,128)(2,1)}, u32[]{:S(2)}) copy-start(bf16[1,32,9,256]{3,1,2,0:T(8,128)(2,1)} %param.9) | copy-start | bytes 442372
  9.8 9.7 %collective-permute-start.4 = (bf16[16,32,256]{2,1,0:T(8,128)(2,1)}, bf16[16,32,256]{2,1,0:T(8,128)(2,1)S(1)}, u32[]{:S(2)}, u32[]{:S(2)}) collective-permute-start(bf16[16,32,256]{2,1,0:T(8,128)(2,1)} %get-tuple-element.37), channel_id=1, source_target_pairs={{8,0},{16,8},{24,16},{9,1},{17,9},{25,17},{10,2},{18,10},{26,18},{... | collective-permute-start | bytes 786440 | tf_op jit(solution)/shard_map/back/ppermute | solution.py:46
  13.4 6.1 %collective-permute-start.2 = (bf16[11,32,256]{2,1,0:T(8,128)(2,1)}, bf16[11,32,256]{2,1,0:T(8,128)(2,1)S(1)}, u32[]{:S(2)}, u32[]{:S(2)}) collective-permute-start(bf16[11,32,256]{2,1,0:T(8,128)(2,1)} %get-tuple-element.34), channel_id=1, source_target_pairs={{0,1},{1,0},{2,3},{3,2},{4,5},{5,4},{6,7},{7,6},{8,9},{9,8},{10,11... | collective-permute-start | bytes 540680 | tf_op jit(solution)/shard_map/lines/ppermute | solution.py:40
  21.0 9.4 %collective-permute-start.5 = (bf16[4,9,32,256]{3,2,1,0:T(8,128)(2,1)S(1)}, bf16[4,9,32,256]{3,2,1,0:T(8,128)(2,1)S(1)}, u32[]{:S(2)}, u32[]{:S(2)}) collective-permute-start(bf16[4,9,32,256]{3,2,1,0:T(8,128)(2,1)S(1)} %get-tuple-element.40), channel_id=1, source_target_pairs={{0,1},{1,0},{2,3},{3,2},{4,5},{5,4},{6,7},{7,6},{8,9},{9,8},{10,11... | collective-permute-start | bytes 1769480 | tf_op jit(solution)/shard_map/term_one/ppermute | solution.py:40
  21.1 9.3 %collective-permute-start.3 = (bf16[16,32,256]{2,1,0:T(8,128)(2,1)S(1)}, bf16[16,32,256]{2,1,0:T(8,128)(2,1)S(1)}, u32[]{:S(2)}, u32[]{:S(2)}) collective-permute-start(bf16[16,32,256]{2,1,0:T(8,128)(2,1)S(1)} %copy-done.7), channel_id=1, source_target_pairs={{0,8},{8,0},{16,24},{24,16},{1,9},{9,1},{17,25},{25,17},{2,10},{10... | collective-permute-start | bytes 786440 | tf_op jit(solution)/shard_map/cross/ppermute | solution.py:46
  23.5 5.9 %collective-permute-start.9 = (bf16[9,32,256]{2,1,0:T(8,128)(2,1)S(1)}, bf16[9,32,256]{2,1,0:T(8,128)(2,1)S(1)}, u32[]{:S(2)}, u32[]{:S(2)}) collective-permute-start(bf16[9,32,256]{2,1,0:T(8,128)(2,1)S(1)} %collective-permute-done.1.rest_2_), channel_id=1, source_target_pairs={{0,2},{1,3},{2,0},{3,1},{4,6},{5,7},{6,4},{7,5},{8,10},{9,11},{10,... | collective-permute-start | bytes 442376 | tf_op jit(solution)/shard_map/weight_z3/ppermute | solution.py:40
  24.0 10.0 %collective-permute-start.8 = (bf16[16,32,256]{2,1,0:T(8,128)(2,1)S(1)}, bf16[16,32,256]{2,1,0:T(8,128)(2,1)S(1)}, u32[]{:S(2)}, u32[]{:S(2)}) collective-permute-start(bf16[16,32,256]{2,1,0:T(8,128)(2,1)S(1)} %copy-done.6), channel_id=1, source_target_pairs={{8,24},{16,0},{9,25},{17,1},{10,26},{18,2},{11,27},{19,3},{12,28},... | collective-permute-start | bytes 786440 | tf_op jit(solution)/shard_map/around_first/ppermute | solution.py:46
  25.3 10.3 %collective-permute-start.10 = (bf16[9,32,256]{2,1,0:T(8,128)(2,1)S(1)}, bf16[9,32,256]{2,1,0:T(8,128)(2,1)S(1)}, u32[]{:S(2)}, u32[]{:S(2)}) collective-permute-start(bf16[9,32,256]{2,1,0:T(8,128)(2,1)S(1)} %bitcast.21), channel_id=1, source_target_pairs={{0,1},{1,0},{2,3},{3,2},{4,5},{5,4},{6,7},{7,6},{8,9},{9,8},{10,11... | collective-permute-start | bytes 442376 | tf_op jit(solution)/shard_map/weight_core0/ppermute | solution.py:40
  29.4 6.1 %collective-permute-start.11 = (bf16[9,32,256]{2,1,0:T(8,128)(2,1)S(1)}, bf16[9,32,256]{2,1,0:T(8,128)(2,1)S(1)}, u32[]{:S(2)}, u32[]{:S(2)}) collective-permute-start(bf16[9,32,256]{2,1,0:T(8,128)(2,1)S(1)} %collective-permute-done.rest_1_), channel_id=1, source_target_pairs={{0,1},{1,0},{2,3},{3,2},{4,5},{5,4},{6,7},{7,6},{8,9},{9,8},{10,11... | collective-permute-start | bytes 442376 | tf_op jit(solution)/shard_map/weight_core1/ppermute | solution.py:40
  30.4 5.1 %collective-permute-start.12 = (bf16[9,32,256]{2,1,0:T(8,128)(2,1)S(1)}, bf16[9,32,256]{2,1,0:T(8,128)(2,1)S(1)}, u32[]{:S(2)}, u32[]{:S(2)}) collective-permute-start(bf16[9,32,256]{2,1,0:T(8,128)(2,1)S(1)} %collective-permute-done.1.rest_2_), channel_id=1, source_target_pairs={{0,1},{1,0},{2,3},{3,2},{4,5},{5,4},{6,7},{7,6},{8,9},{9,8},{10,11... | collective-permute-start | bytes 442376 | tf_op jit(solution)/shard_map/weight_core2/ppermute | solution.py:40
  30.4 5.1 %collective-permute-start.13 = (bf16[9,32,256]{2,1,0:T(8,128)(2,1)S(1)}, bf16[9,32,256]{2,1,0:T(8,128)(2,1)S(1)}, u32[]{:S(2)}, u32[]{:S(2)}) collective-permute-start(bf16[9,32,256]{2,1,0:T(8,128)(2,1)S(1)} %collective-permute-done.9.rest_3_), channel_id=1, source_target_pairs={{0,1},{1,0},{2,3},{3,2},{4,5},{5,4},{6,7},{7,6},{8,9},{9,8},{10,11... | collective-permute-start | bytes 442376 | tf_op jit(solution)/shard_map/weight_core3/ppermute | solution.py:40
  34.0 7.9 %collective-permute-start.6 = (bf16[2,9,32,256]{3,2,1,0:T(8,128)(2,1)S(1)}, bf16[2,9,32,256]{3,2,1,0:T(8,128)(2,1)S(1)}, u32[]{:S(2)}, u32[]{:S(2)}) collective-permute-start(bf16[2,9,32,256]{3,2,1,0:T(8,128)(2,1)S(1)} %get-tuple-element.42), channel_id=1, source_target_pairs={{0,2},{1,3},{2,0},{3,1},{4,6},{5,7},{6,4},{7,5},{8,10},{9,11},{10,... | collective-permute-start | bytes 884744 | tf_op jit(solution)/shard_map/term_one_near/ppermute | solution.py:40
  43.9 2.1 %collective-permute-start.14 = (bf16[4,9,32,256]{3,2,1,0:T(8,128)(2,1)S(1)}, bf16[4,9,32,256]{3,2,1,0:T(8,128)(2,1)S(1)}, u32[]{:S(2)}, u32[]{:S(2)}) collective-permute-start(bf16[4,9,32,256]{3,2,1,0:T(8,128)(2,1)S(1)} %get-tuple-element.52), channel_id=1, source_target_pairs={{0,1},{1,0},{2,3},{3,2},{4,5},{5,4},{6,7},{7,6},{8,9},{9,8},{10,11... | collective-permute-start | bytes 1769480 | tf_op jit(solution)/shard_map/term_two/ppermute | solution.py:40
  44.0 18.4 %collective-permute-start.19 = (bf16[2,544,256]{2,1,0:T(8,128)(2,1)S(1)}, bf16[2,544,256]{2,1,0:T(8,128)(2,1)S(1)}, u32[]{:S(2)}, u32[]{:S(2)}) collective-permute-start(bf16[2,544,256]{2,1,0:T(8,128)(2,1)S(1)} %get-tuple-element.50.message), channel_id=1, source_target_pairs={{8,0},{16,8},{24,16},{9,1},{17,9},{25,17},{10,2},{18,10},{26,18},{... | collective-permute-start | bytes 1671176 | tf_op jit(solution)/shard_map/late_back/ppermute | solution.py:46
  46.6 15.0 %collective-permute-start.15 = (bf16[2,9,32,256]{3,2,1,0:T(8,128)(2,1)S(1)}, bf16[2,9,32,256]{3,2,1,0:T(8,128)(2,1)S(1)}, u32[]{:S(2)}, u32[]{:S(2)}) collective-permute-start(bf16[2,9,32,256]{3,2,1,0:T(8,128)(2,1)S(1)} %get-tuple-element.54), channel_id=1, source_target_pairs={{0,2},{1,3},{2,0},{3,1},{4,6},{5,7},{6,4},{7,5},{8,10},{9,11},{10,... | collective-permute-start | bytes 884744 | tf_op jit(solution)/shard_map/term_two_near/ppermute | solution.py:40
  48.3 14.1 %collective-permute-start.17 = (bf16[16,32,256]{2,1,0:T(8,128)(2,1)S(1)}, bf16[16,32,256]{2,1,0:T(8,128)(2,1)S(1)}, u32[]{:S(2)}, u32[]{:S(2)}) collective-permute-start(bf16[16,32,256]{2,1,0:T(8,128)(2,1)S(1)} %collective-permute-done.8), channel_id=1, source_target_pairs={{0,8},{24,16},{1,9},{25,17},{2,10},{26,18},{3,11},{27,19},{4,12},{... | collective-permute-start | bytes 786440 | tf_op jit(solution)/shard_map/around_second/ppermute | solution.py:46
  52.2 9.5 %collective-permute-start.7 = (bf16[1,9,32,256]{3,2,1,0:T(8,128)(2,1)S(1)}, bf16[1,9,32,256]{3,2,1,0:T(8,128)(2,1)S(1)}, u32[]{:S(2)}, u32[]{:S(2)}) collective-permute-start(bf16[1,9,32,256]{3,2,1,0:T(8,128)(2,1)S(1)} %get-tuple-element.43), channel_id=1, source_target_pairs={{0,4},{1,5},{2,6},{3,7},{4,0},{5,1},{6,2},{7,3},{8,12},{9,13},{10,... | collective-permute-start | bytes 442376 | tf_op jit(solution)/shard_map/term_one_far/ppermute | solution.py:40
  52.6 18.1 %collective-permute-start.18 = (bf16[544,256]{1,0:T(8,128)(2,1)S(1)}, bf16[544,256]{1,0:T(8,128)(2,1)S(1)}, u32[]{:S(2)}, u32[]{:S(2)}) collective-permute-start(bf16[544,256]{1,0:T(8,128)(2,1)S(1)} %get-tuple-element.59.own_second), channel_id=1, source_target_pairs={{0,8},{8,16},{16,24},{1,9},{9,17},{17,25},{2,10},{10,18},{18,26},{... | collective-permute-start | bytes 835592 | tf_op jit(solution)/shard_map/late_fwd/ppermute | solution.py:46
  62.3 6.5 %collective-permute-start.16 = (bf16[1,9,32,256]{3,2,1,0:T(8,128)(2,1)S(1)}, bf16[1,9,32,256]{3,2,1,0:T(8,128)(2,1)S(1)}, u32[]{:S(2)}, u32[]{:S(2)}) collective-permute-start(bf16[1,9,32,256]{3,2,1,0:T(8,128)(2,1)S(1)} %get-tuple-element.56), channel_id=1, source_target_pairs={{0,4},{1,5},{2,6},{3,7},{4,0},{5,1},{6,2},{7,3},{8,12},{9,13},{10,... | collective-permute-start | bytes 442376 | tf_op jit(solution)/shard_map/term_two_far/ppermute | solution.py:40
  62.4 8.3 %copy-start.3 = (bf16[2,1,16,32,256]{4,3,2,1,0:T(8,128)(2,1)S(1)}, bf16[2,1,16,32,256]{4,3,2,1,0:T(8,128)(2,1)}, u32[]{:S(2)}) copy-start(bf16[2,1,16,32,256]{4,3,2,1,0:T(8,128)(2,1)} %fresh.3) | copy-start | bytes 1572868
  69.4 7.7 %collective-permute-start.20 = (bf16[9,32,256]{2,1,0:T(8,128)(2,1)S(1)}, bf16[9,32,256]{2,1,0:T(8,128)(2,1)S(1)}, u32[]{:S(2)}, u32[]{:S(2)}) collective-permute-start(bf16[9,32,256]{2,1,0:T(8,128)(2,1)S(1)} %gather_sum_kernel.1), channel_id=1, source_target_pairs={{8,0},{16,8},{24,16},{9,1},{17,9},{25,17},{10,2},{18,10},{26,18},{... | collective-permute-start | bytes 442376 | tf_op jit(solution)/shard_map/below/ppermute | solution.py:46

commit v3 on v1

--- a/solution.py
+++ b/solution.py
@@ -306,6 +306,8 @@
         COLLECT * conv_flops,
         limit=60,
     )
+    if direct:
+        lines = after(lines, *mine[1:-1])
     lines = swapped(lines, 1, "lines")
     back = passed_along(back, -1, "back")
     around = moved(around, "around_first", lambda i: i + 2 if i % 2 else i - 2)
@@ -334,7 +336,6 @@
     terms_one = grads(grad_one_kernel, (after(info, back), lines, fwd_in, bwd_in, top_cot), GRAD_ONE * conv_flops)
     if direct:
         others = mine[:-1] + [after(mine[-1], terms_one[0])]
-        others[1] = after(others[1], mine[-1])
         pieces = mine + [swapped(x, 1, "weight_core%d" % k) for k, x in enumerate(others)]
         cross = after(cross, pieces[-2])
     else:
@@ -345,7 +346,7 @@
     message, second, weight = call(
         step_one_kernel,
         (taller(2), taller(), jax.ShapeDtypeStruct((TAPS, channels, outs), BF16)),
-        (after(info, around, cross), lines, fwd_in, bwd_in, *pieces),
+        (after(info, around), lines, fwd_in, bwd_in, *pieces),
         1,
         [ext],
     )
@@ -355,7 +356,7 @@
     turn = lambda i: i ^ 1 if (i >= 2 if i % 2 else i <= last - 2) else -1
     around = moved(after(around, message), "around_second", turn)
 
-    terms_two = grads(functools.partial(grad_two_kernel, height, width), (info, message), 1)
+    terms_two = grads(functools.partial(grad_two_kernel, height, width), (after(info, cross), message), 1)
     own_one, parts_one = scattered("term_one", *terms_one)
     own_two, parts_two = scattered("term_two", *terms_two)
     below = call(gather_sum_kernel, like(shard, BF16), (info, own_two, *parts_two))

time: 65.7 us -> 64.5 us (0.982); the launches traced: 65.4 us -> 63.3 us
  waiting for transfers between devices: 16.7 us -> 13.8 us
  starting transfers between devices: 29.2 us -> 29.9 us
    ppermute x7, waiting for transfers between devices: 9.21 us -> 7.32 us  [moved(): lax.ppermute(block, 'segment', [(i, target(i)) for i in devices if target...]
    ppermute x7, starting transfers between devices: 16.6 us -> 17.6 us  [moved(): lax.ppermute(block, 'segment', [(i, target(i)) for i in devices if target...]
    ppermute x14, waiting for transfers between devices: 7.46 us -> 6.52 us  [swapped(): lax.ppermute(x, 'dp', [(i, i ^ bit) for i in range(lax.axis_size('dp'))])]
  transfers between devices with their start and end apart: 21 -> 21, of which waited for: 9 -> 9; matrix products, arithmetic and copies ran while one was open for 1% -> 1% of each run, Pallas kernels for 19% -> 24%
where the time goes in v3:
time: 64.5 us; the launch traced here: 63.3 us
  starting transfers between devices  29.9 us (46%)
  Pallas kernels  18 us (28%)
  waiting for transfers between devices  13.8 us (21%)
  between operations  0.83 us (1%)
  local copies, waits for them, and re-layouts  0.68 us (1%)
    pallas_call x12, Pallas kernels, call(): pl.pallas_call(kernel, name=name, out_shape=out_shape, in_specs=[SMEM] +...  18 us
    ppermute x7, starting transfers between devices, moved(): lax.ppermute(block, 'segment', [(i, target(i)) for i in devices if target...  17.6 us
    ppermute x14, starting transfers between devices, swapped(): lax.ppermute(x, 'dp', [(i, i ^ bit) for i in range(lax.axis_size('dp'))])  12.3 us
    ppermute x7, waiting for transfers between devices, moved(): lax.ppermute(block, 'segment', [(i, target(i)) for i in devices if target...  7.32 us
    ppermute x14, waiting for transfers between devices, swapped(): lax.ppermute(x, 'dp', [(i, i ^ bit) for i in range(lax.axis_size('dp'))])  6.52 us
  transfers between devices with their start and end apart: 21, of which 9 were waited for; matrix products, arithmetic and copies ran while one was open for 1% of the time, Pallas kernels for 24%

profile of v3, /device:TPU:0, one launch (start us, length us, event | category | flops | bytes accessed | tf_op | source)
XLA Modules:
  0.0 63.3 jit_solution(9900990037008758085)
XLA Ops:
  0.6 4.1 %collective-permute-start.1 = (bf16[9,32,256]{2,1,0:T(8,128)(2,1)}, bf16[9,32,256]{2,1,0:T(8,128)(2,1)S(1)}, u32[]{:S(2)}, u32[]{:S(2)}) collective-permute-start(bf16[9,32,256]{2,1,0:T(8,128)(2,1)} %bitcast.17), channel_id=1, source_target_pairs={{0,4},{1,5},{2,6},{3,7},{4,0},{5,1},{6,2},{7,3},{8,12},{9,13},{10,... | collective-permute-start | bytes 442376 | tf_op jit(solution)/shard_map/weight_z2/ppermute | solution.py:39
  4.7 1.6 %collective-permute-start = (bf16[9,32,256]{2,1,0:T(8,128)(2,1)}, bf16[9,32,256]{2,1,0:T(8,128)(2,1)S(1)}, u32[]{:S(2)}, u32[]{:S(2)}) collective-permute-start(bf16[9,32,256]{2,1,0:T(8,128)(2,1)} %bitcast.18), channel_id=1, source_target_pairs={{0,2},{1,3},{2,0},{3,1},{4,6},{5,7},{6,4},{7,5},{8,10},{9,11},{10,... | collective-permute-start | bytes 442376 | tf_op jit(solution)/shard_map/weight_z1/ppermute | solution.py:39
  6.3 0.7 %stack.31.info = s32[5]{0:T(128)} concatenate(s32[1]{0:T(128)} %bitcast, s32[1]{0:T(128)} %bitcast.1, s32[1]{0:T(128)} %bitcast.2, s32[1]{0:T(128)} %bitcast.3, s32[1]{0:T(128)} %bitcast.4), dimensions={0} | concatenate | bytes 40 | tf_op jit(solution)/shard_map/stack | solution.py:281
  7.0 0.0 copy-start.4
  7.0 0.0 copy-start
  7.0 0.0 copy-start.5
  7.0 2.8 %collect_kernel.1 = (bf16[11,32,256]{2,1,0:T(8,128)(2,1)}, bf16[16,32,256]{2,1,0:T(8,128)(2,1)}, bf16[16,32,256]{2,1,0:T(8,128)(2,1)}, bf16[16,32,256]{2,1,0:T(8,128)(2,1)}) custom-call(s32[5]{0:T(128)} %stack.31.info, bf16[2,1,1,16,32,256]{5,4,3,2,1,0:T(8,128)(2,1)} %fwd_in.7, bf16[4,1,1,16,32,256]{5,4,3,2,1,0:T(8,128)(2,1)} %bwd_in.5, ...), custom_call_target="tpu_custom_call" | custom-call | bytes 1 | tf_op jit(solution)/shard_map/collect_kernel/pallas_call | solution.py:25
  9.8 1.3 %collective-permute-start.9 = (bf16[16,32,256]{2,1,0:T(8,128)(2,1)}, bf16[16,32,256]{2,1,0:T(8,128)(2,1)S(1)}, u32[]{:S(2)}, u32[]{:S(2)}) collective-permute-start(bf16[16,32,256]{2,1,0:T(8,128)(2,1)} %get-tuple-element.35), channel_id=1, source_target_pairs={{8,0},{16,8},{24,16},{9,1},{17,9},{25,17},{10,2},{18,10},{26,18},{... | collective-permute-start | bytes 786440 | tf_op jit(solution)/shard_map/back/ppermute | solution.py:45
  11.1 1.0 %collective-permute-done.1.rest_2_ = bf16[9,32,256]{2,1,0:T(8,128)(2,1)S(1)} collective-permute-done((bf16[9,32,256]{2,1,0:T(8,128)(2,1)}, bf16[9,32,256]{2,1,0:T(8,128)(2,1)S(1)}, u32[]{:S(2)}, u32[]{:S(2)}) %collective-permute-start.1) | collective-permute-done | bytes 147488 | tf_op jit(solution)/shard_map/weight_z2/ppermute | solution.py:39
  12.1 0.0 collective-permute-start.3
  12.1 0.2 collective-permute-done.rest_1_
  12.2 0.3 collective-permute-start.2
  12.6 1.2 %collective-permute-start.6 = (bf16[9,32,256]{2,1,0:T(8,128)(2,1)S(1)}, bf16[9,32,256]{2,1,0:T(8,128)(2,1)S(1)}, u32[]{:S(2)}, u32[]{:S(2)}) collective-permute-start(bf16[9,32,256]{2,1,0:T(8,128)(2,1)S(1)} %collective-permute-done.1.rest_2_), channel_id=1, source_target_pairs={{0,2},{1,3},{2,0},{3,1},{4,6},{5,7},{6,4},{7,5},{8,10},{9,11},{10,... | collective-permute-start | bytes 442376 | tf_op jit(solution)/shard_map/weight_z3/ppermute | solution.py:39
  13.7 1.3 %collective-permute-start.5 = (bf16[16,32,256]{2,1,0:T(8,128)(2,1)}, bf16[16,32,256]{2,1,0:T(8,128)(2,1)S(1)}, u32[]{:S(2)}, u32[]{:S(2)}) collective-permute-start(bf16[16,32,256]{2,1,0:T(8,128)(2,1)} %get-tuple-element.33), channel_id=1, source_target_pairs={{8,24},{16,0},{9,25},{17,1},{10,26},{18,2},{11,27},{19,3},{12,28},... | collective-permute-start | bytes 786440 | tf_op jit(solution)/shard_map/around_first/ppermute | solution.py:45
  15.0 0.0 collective-permute-done.3.rest_6_
  15.0 3.7 %collective-permute-start.4 = (bf16[16,32,256]{2,1,0:T(8,128)(2,1)}, bf16[16,32,256]{2,1,0:T(8,128)(2,1)S(1)}, u32[]{:S(2)}, u32[]{:S(2)}) collective-permute-start(bf16[16,32,256]{2,1,0:T(8,128)(2,1)} %get-tuple-element.32), channel_id=1, source_target_pairs={{0,8},{8,0},{16,24},{24,16},{1,9},{9,1},{17,25},{25,17},{2,10},{10... | collective-permute-start | bytes 786440 | tf_op jit(solution)/shard_map/cross/ppermute | solution.py:45
  18.7 0.6 collective-permute-done.9.back
  19.4 0.0 copy-done.4
  19.4 0.0 collective-permute-start.7
  19.4 0.0 collective-permute-done.2.lines
  19.4 0.5 collective-permute-start.8
  19.9 0.0 copy-done
  19.9 0.0 copy-done.1
  19.9 0.0 copy-done.2
  19.9 0.0 copy-done.5
  19.9 1.4 %grad_one_kernel.1 = (f32[4,9,32,256]{3,2,1,0:T(8,128)S(1)}, bf16[4,9,32,256]{3,2,1,0:T(8,128)(2,1)S(1)}) custom-call(s32[5]{0:T(128)S(1)} %copy-done.5, bf16[11,32,256]{2,1,0:T(8,128)(2,1)S(1)} %collective-permute-done.2.lines, bf16[2,1,1,16,32,256]{5,4,3,2,1,0:T(8,128)(2,1)S(1)} %copy-done.1, bf16[4,1,1,16,32,256]{5,4,3,2,1,0:T(8,128)(2,1)S(1)} %copy-done, ...), custom_call_target="tpu_custom_call" | custom-call | bytes 1 | tf_op jit(solution)/shard_map/grad_one_kernel/pallas_call | solution.py:25
  21.3 0.0 collective-permute-done.6.rest_3_
  21.4 0.1 collective-permute-start.10
  21.5 2.8 %collective-permute-done.5 = bf16[16,32,256]{2,1,0:T(8,128)(2,1)S(1)} collective-permute-done((bf16[16,32,256]{2,1,0:T(8,128)(2,1)}, bf16[16,32,256]{2,1,0:T(8,128)(2,1)S(1)}, u32[]{:S(2)}, u32[]{:S(2)}) %collective-permute-start.5) | collective-permute-done | bytes 262176 | tf_op jit(solution)/shard_map/around_first/ppermute | solution.py:45
  24.3 0.0 collective-permute-done.7.rest_4_
  24.3 0.0 collective-permute-done.8.rest_5_
  24.3 0.0 collective-permute-done.10.rest_7_
  24.3 2.9 %step_one_kernel.1 = (bf16[2,544,256]{2,1,0:T(8,128)(2,1)S(1)}, bf16[544,256]{1,0:T(8,128)(2,1)S(1)}, bf16[9,256,256]{2,1,0:T(8,128)(2,1)S(1)}) custom-call(s32[5]{0:T(128)S(1)} %copy-done.5, bf16[11,32,256]{2,1,0:T(8,128)(2,1)S(1)} %collective-permute-done.2.lines, bf16[2,1,1,16,32,256]{5,4,3,2,1,0:T(8,128)(2,1)S(1)} %copy-done.1, ...), custom_call_target="tpu_custom_call" | custom-call | flops 1 | bytes 1 | tf_op jit(solution)/shard_map/step_one_kernel/pallas_call | solution.py:25
  27.2 0.0 collective-permute-done.4.cross
  27.2 1.4 %grad_two_kernel.1 = (f32[4,9,32,256]{3,2,1,0:T(8,128)S(1)}, bf16[4,9,32,256]{3,2,1,0:T(8,128)(2,1)S(1)}) custom-call(s32[5]{0:T(128)S(1)} %copy-done.5, bf16[2,544,256]{2,1,0:T(8,128)(2,1)S(1)} %get-tuple-element.39.message), custom_call_target="tpu_custom_call" | custom-call | flops 1 | bytes 1 | tf_op jit(solution)/shard_map/grad_two_kernel/pallas_call | solution.py:25
  28.6 0.1 collective-permute-start.17
  28.7 0.5 collective-permute-start.14
  29.2 1.3 %collective-permute-start.13 = (bf16[2,544,256]{2,1,0:T(8,128)(2,1)S(1)}, bf16[2,544,256]{2,1,0:T(8,128)(2,1)S(1)}, u32[]{:S(2)}, u32[]{:S(2)}) collective-permute-start(bf16[2,544,256]{2,1,0:T(8,128)(2,1)S(1)} %get-tuple-element.39.message), channel_id=1, source_target_pairs={{8,0},{16,8},{24,16},{9,1},{17,9},{25,17},{10,2},{18,10},{26,18},{... | collective-permute-start | bytes 1671176 | tf_op jit(solution)/shard_map/late_back/ppermute | solution.py:45
  30.5 0.2 collective-permute-done.17.got
  30.7 0.6 %pair_sum_kernel.3 = (f32[2,9,32,256]{3,2,1,0:T(8,128)S(1)}, bf16[2,9,32,256]{3,2,1,0:T(8,128)(2,1)S(1)}) custom-call(s32[5]{0:T(128)S(1)} %copy-done.5, f32[4,9,32,256]{3,2,1,0:T(8,128)S(1)} %get-tuple-element.49.keep, bf16[4,9,32,256]{3,2,1,0:T(8,128)(2,1)S(1)} %collective-permute-done.17.got), custom_call_target="tpu_custom_call" | custom-call | bytes 1 | tf_op jit(solution)/shard_map/pair_sum_kernel/pallas_call | solution.py:25
  31.3 0.8 %collective-permute-start.18 = (bf16[2,9,32,256]{3,2,1,0:T(8,128)(2,1)S(1)}, bf16[2,9,32,256]{3,2,1,0:T(8,128)(2,1)S(1)}, u32[]{:S(2)}, u32[]{:S(2)}) collective-permute-start(bf16[2,9,32,256]{3,2,1,0:T(8,128)(2,1)S(1)} %get-tuple-element.52), channel_id=1, source_target_pairs={{0,2},{1,3},{2,0},{3,1},{4,6},{5,7},{6,4},{7,5},{8,10},{9,11},{10,... | collective-permute-start | bytes 884744 | tf_op jit(solution)/shard_map/term_two_near/ppermute | solution.py:39
  32.1 4.5 %collective-permute-start.12 = (bf16[544,256]{1,0:T(8,128)(2,1)S(1)}, bf16[544,256]{1,0:T(8,128)(2,1)S(1)}, u32[]{:S(2)}, u32[]{:S(2)}) collective-permute-start(bf16[544,256]{1,0:T(8,128)(2,1)S(1)} %get-tuple-element.41.own_second), channel_id=1, source_target_pairs={{0,8},{8,16},{16,24},{1,9},{9,17},{17,25},{2,10},{10,18},{18,26},{... | collective-permute-start | bytes 835592 | tf_op jit(solution)/shard_map/late_fwd/ppermute | solution.py:45
  36.6 4.3 %collective-permute-start.11 = (bf16[16,32,256]{2,1,0:T(8,128)(2,1)S(1)}, bf16[16,32,256]{2,1,0:T(8,128)(2,1)S(1)}, u32[]{:S(2)}, u32[]{:S(2)}) collective-permute-start(bf16[16,32,256]{2,1,0:T(8,128)(2,1)S(1)} %collective-permute-done.5), channel_id=1, source_target_pairs={{0,8},{24,16},{1,9},{25,17},{2,10},{26,18},{3,11},{27,19},{4,12},{... | collective-permute-start | bytes 786440 | tf_op jit(solution)/shard_map/around_second/ppermute | solution.py:45
  40.9 0.0 collective-permute-done.14.got
  40.9 0.6 %pair_sum_kernel.2 = (f32[2,9,32,256]{3,2,1,0:T(8,128)S(1)}, bf16[2,9,32,256]{3,2,1,0:T(8,128)(2,1)S(1)}) custom-call(s32[5]{0:T(128)S(1)} %copy-done.5, f32[4,9,32,256]{3,2,1,0:T(8,128)S(1)} %get-tuple-element.37.keep, bf16[4,9,32,256]{3,2,1,0:T(8,128)(2,1)S(1)} %collective-permute-done.14.got), custom_call_target="tpu_custom_call" | custom-call | bytes 1 | tf_op jit(solution)/shard_map/pair_sum_kernel/pallas_call | solution.py:25
  41.6 1.9 %collective-permute-start.15 = (bf16[2,9,32,256]{3,2,1,0:T(8,128)(2,1)S(1)}, bf16[2,9,32,256]{3,2,1,0:T(8,128)(2,1)S(1)}, u32[]{:S(2)}, u32[]{:S(2)}) collective-permute-start(bf16[2,9,32,256]{3,2,1,0:T(8,128)(2,1)S(1)} %get-tuple-element.45), channel_id=1, source_target_pairs={{0,2},{1,3},{2,0},{3,1},{4,6},{5,7},{6,4},{7,5},{8,10},{9,11},{10,... | collective-permute-start | bytes 884744 | tf_op jit(solution)/shard_map/term_one_near/ppermute | solution.py:39
  43.5 0.0 collective-permute-done.18.got
  43.5 0.6 fold_kernel.3
  44.1 1.0 %collective-permute-start.19 = (bf16[1,9,32,256]{3,2,1,0:T(8,128)(2,1)S(1)}, bf16[1,9,32,256]{3,2,1,0:T(8,128)(2,1)S(1)}, u32[]{:S(2)}, u32[]{:S(2)}) collective-permute-start(bf16[1,9,32,256]{3,2,1,0:T(8,128)(2,1)S(1)} %get-tuple-element.54), channel_id=1, source_target_pairs={{0,4},{1,5},{2,6},{3,7},{4,0},{5,1},{6,2},{7,3},{8,12},{9,13},{10,... | collective-permute-start | bytes 442376 | tf_op jit(solution)/shard_map/term_two_far/ppermute | solution.py:39
  45.1 2.7 %collective-permute-done.11.around = bf16[16,32,256]{2,1,0:T(8,128)(2,1)S(1)} collective-permute-done((bf16[16,32,256]{2,1,0:T(8,128)(2,1)S(1)}, bf16[16,32,256]{2,1,0:T(8,128)(2,1)S(1)}, u32[]{:S(2)}, u32[]{:S(2)}) %collective-permute-start.11) | collective-permute-done | bytes 262176 | tf_op jit(solution)/shard_map/around_second/ppermute | solution.py:45
  47.8 0.0 collective-permute-done.12.second
  47.8 0.0 copy-done.3
  47.8 2.2 %forward_two_kernel.1 = bf16[2,1,1,16,32,256]{5,4,3,2,1,0:T(8,128)(2,1)} custom-call(s32[5]{0:T(128)S(1)} %copy-done.5, bf16[11,32,256]{2,1,0:T(8,128)(2,1)S(1)} %collective-permute-done.2.lines, bf16[16,32,256]{2,1,0:T(8,128)(2,1)S(1)} %collective-permute-done.4.cross, bf16[16,32,256]{2,1,0:T(8,128)(2,1)S(1)} %collective-permute-done.11.around, ...), custom_call_target="tpu_custom_call" | custom-call | flops 1811939328 | bytes 1 | tf_op jit(solution)/shard_map/forward_two_kernel/pallas_call | solution.py:25
  50.0 2.9 %collective-permute-done.15.got = bf16[2,9,32,256]{3,2,1,0:T(8,128)(2,1)S(1)} collective-permute-done((bf16[2,9,32,256]{3,2,1,0:T(8,128)(2,1)S(1)}, bf16[2,9,32,256]{3,2,1,0:T(8,128)(2,1)S(1)}, u32[]{:S(2)}, u32[]{:S(2)}) %collective-permute-start.15) | collective-permute-done | bytes 294944 | tf_op jit(solution)/shard_map/term_one_near/ppermute | solution.py:39
  52.8 0.6 fold_kernel.2
  53.4 0.2 collective-permute-start.16
  53.6 0.0 collective-permute-done.19
  53.6 0.6 gather_sum_kernel.1
  54.2 1.3 %collective-permute-start.20 = (bf16[9,32,256]{2,1,0:T(8,128)(2,1)S(1)}, bf16[9,32,256]{2,1,0:T(8,128)(2,1)S(1)}, u32[]{:S(2)}, u32[]{:S(2)}) collective-permute-start(bf16[9,32,256]{2,1,0:T(8,128)(2,1)S(1)} %gather_sum_kernel.1), channel_id=1, source_target_pairs={{8,0},{16,8},{24,16},{9,1},{17,9},{25,17},{10,2},{18,10},{26,18},{... | collective-permute-start | bytes 442376 | tf_op jit(solution)/shard_map/below/ppermute | solution.py:45
  55.5 0.0 collective-permute-done.13.message
  55.5 3.0 %backward_two_kernel.1 = bf16[4,1,1,16,32,256]{5,4,3,2,1,0:T(8,128)(2,1)} custom-call(s32[5]{0:T(128)S(1)} %copy-done.5, bf16[11,32,256]{2,1,0:T(8,128)(2,1)S(1)} %collective-permute-done.2.lines, bf16[16,32,256]{2,1,0:T(8,128)(2,1)S(1)} %collective-permute-done.9.back, bf16[16,32,256]{2,1,0:T(8,128)(2,1)S(1)} %collective-permute-done.4.cross, ...), custom_call_target="tpu_custom_call" | custom-call | flops 1811939328 | bytes 1 | tf_op jit(solution)/shard_map/backward_two_kernel/pallas_call | solution.py:25
  58.5 2.2 %collective-permute-done.16 = bf16[1,9,32,256]{3,2,1,0:T(8,128)(2,1)S(1)} collective-permute-done((bf16[1,9,32,256]{3,2,1,0:T(8,128)(2,1)S(1)}, bf16[1,9,32,256]{3,2,1,0:T(8,128)(2,1)S(1)}, u32[]{:S(2)}, u32[]{:S(2)}) %collective-permute-start.16) | collective-permute-done | bytes 147488 | tf_op jit(solution)/shard_map/term_one_far/ppermute | solution.py:39
  60.7 1.2 %collective-permute-done.20.rest_1_ = bf16[9,32,256]{2,1,0:T(8,128)(2,1)S(1)} collective-permute-done((bf16[9,32,256]{2,1,0:T(8,128)(2,1)S(1)}, bf16[9,32,256]{2,1,0:T(8,128)(2,1)S(1)}, u32[]{:S(2)}, u32[]{:S(2)}) %collective-permute-start.20) | collective-permute-done | bytes 147488 | tf_op jit(solution)/shard_map/below/ppermute | solution.py:45
  62.0 1.3 %finish_kernel.1 = f32[9,32,256]{2,1,0:T(8,128)} custom-call(s32[5]{0:T(128)S(1)} %copy-done.5, f32[9,32,256]{2,1,0:T(8,128)S(1)} %bitcast.15, bf16[9,32,256]{2,1,0:T(8,128)(2,1)S(1)} %bitcast.21, bf16[9,32,256]{2,1,0:T(8,128)(2,1)S(1)} %collective-permute-done.20.rest_1_), custom_call_target="tpu_custom_call" | custom-call | bytes 1 | tf_op jit(solution)/shard_map/finish_kernel/pallas_call | solution.py:25
  (3 shorter events, 0.0 us)
Async XLA Ops:
  0.6 11.4 %collective-permute-start.1 = (bf16[9,32,256]{2,1,0:T(8,128)(2,1)}, bf16[9,32,256]{2,1,0:T(8,128)(2,1)S(1)}, u32[]{:S(2)}, u32[]{:S(2)}) collective-permute-start(bf16[9,32,256]{2,1,0:T(8,128)(2,1)} %bitcast.17), channel_id=1, source_target_pairs={{0,4},{1,5},{2,6},{3,7},{4,0},{5,1},{6,2},{7,3},{8,12},{9,13},{10,... | collective-permute-start | bytes 442376 | tf_op jit(solution)/shard_map/weight_z2/ppermute | solution.py:39
  4.7 7.5 %collective-permute-start = (bf16[9,32,256]{2,1,0:T(8,128)(2,1)}, bf16[9,32,256]{2,1,0:T(8,128)(2,1)S(1)}, u32[]{:S(2)}, u32[]{:S(2)}) collective-permute-start(bf16[9,32,256]{2,1,0:T(8,128)(2,1)} %bitcast.18), channel_id=1, source_target_pairs={{0,2},{1,3},{2,0},{3,1},{4,6},{5,7},{6,4},{7,5},{8,10},{9,11},{10,... | collective-permute-start | bytes 442376 | tf_op jit(solution)/shard_map/weight_z1/ppermute | solution.py:39
  7.0 12.4 %copy-start.4 = (bf16[1,32,9,256]{3,1,2,0:T(8,128)(2,1)S(1)}, bf16[1,32,9,256]{3,1,2,0:T(8,128)(2,1)}, u32[]{:S(2)}) copy-start(bf16[1,32,9,256]{3,1,2,0:T(8,128)(2,1)} %param.9) | copy-start | bytes 442372
  7.0 12.9 %copy-start = (bf16[4,1,1,16,32,256]{5,4,3,2,1,0:T(8,128)(2,1)S(1)}, bf16[4,1,1,16,32,256]{5,4,3,2,1,0:T(8,128)(2,1)}, u32[]{:S(2)}) copy-start(bf16[4,1,1,16,32,256]{5,4,3,2,1,0:T(8,128)(2,1)} %bwd_in.5) | copy-start | bytes 3145732
  7.0 12.9 %copy-start.1 = (bf16[2,1,1,16,32,256]{5,4,3,2,1,0:T(8,128)(2,1)S(1)}, bf16[2,1,1,16,32,256]{5,4,3,2,1,0:T(8,128)(2,1)}, u32[]{:S(2)}) copy-start(bf16[2,1,1,16,32,256]{5,4,3,2,1,0:T(8,128)(2,1)} %fwd_in.7) | copy-start | bytes 1572868
  7.0 12.9 %copy-start.2 = (bf16[2,1,16,32,256]{4,3,2,1,0:T(8,128)(2,1)S(1)}, bf16[2,1,16,32,256]{4,3,2,1,0:T(8,128)(2,1)}, u32[]{:S(2)}) copy-start(bf16[2,1,16,32,256]{4,3,2,1,0:T(8,128)(2,1)} %top_cot.5) | copy-start | bytes 1572868
  7.0 12.9 %copy-start.5 = (s32[5]{0:T(128)S(1)}, s32[5]{0:T(128)}, u32[]{:S(2)}) copy-start(s32[5]{0:T(128)} %stack.31.info) | copy-start | bytes 64
  9.8 9.6 %collective-permute-start.9 = (bf16[16,32,256]{2,1,0:T(8,128)(2,1)}, bf16[16,32,256]{2,1,0:T(8,128)(2,1)S(1)}, u32[]{:S(2)}, u32[]{:S(2)}) collective-permute-start(bf16[16,32,256]{2,1,0:T(8,128)(2,1)} %get-tuple-element.35), channel_id=1, source_target_pairs={{8,0},{16,8},{24,16},{9,1},{17,9},{25,17},{10,2},{18,10},{26,18},{... | collective-permute-start | bytes 786440 | tf_op jit(solution)/shard_map/back/ppermute | solution.py:45
  12.1 3.0 %collective-permute-start.3 = (bf16[9,32,256]{2,1,0:T(8,128)(2,1)S(1)}, bf16[9,32,256]{2,1,0:T(8,128)(2,1)S(1)}, u32[]{:S(2)}, u32[]{:S(2)}) collective-permute-start(bf16[9,32,256]{2,1,0:T(8,128)(2,1)S(1)} %collective-permute-done.1.rest_2_), channel_id=1, source_target_pairs={{0,1},{1,0},{2,3},{3,2},{4,5},{5,4},{6,7},{7,6},{8,9},{9,8},{10,11... | collective-permute-start | bytes 442376 | tf_op jit(solution)/shard_map/weight_core2/ppermute | solution.py:39
  12.2 7.1 %collective-permute-start.2 = (bf16[11,32,256]{2,1,0:T(8,128)(2,1)}, bf16[11,32,256]{2,1,0:T(8,128)(2,1)S(1)}, u32[]{:S(2)}, u32[]{:S(2)}) collective-permute-start(bf16[11,32,256]{2,1,0:T(8,128)(2,1)} %get-tuple-element.30), channel_id=1, source_target_pairs={{0,1},{1,0},{2,3},{3,2},{4,5},{5,4},{6,7},{7,6},{8,9},{9,8},{10,11... | collective-permute-start | bytes 540680 | tf_op jit(solution)/shard_map/lines/ppermute | solution.py:39
  12.6 8.8 %collective-permute-start.6 = (bf16[9,32,256]{2,1,0:T(8,128)(2,1)S(1)}, bf16[9,32,256]{2,1,0:T(8,128)(2,1)S(1)}, u32[]{:S(2)}, u32[]{:S(2)}) collective-permute-start(bf16[9,32,256]{2,1,0:T(8,128)(2,1)S(1)} %collective-permute-done.1.rest_2_), channel_id=1, source_target_pairs={{0,2},{1,3},{2,0},{3,1},{4,6},{5,7},{6,4},{7,5},{8,10},{9,11},{10,... | collective-permute-start | bytes 442376 | tf_op jit(solution)/shard_map/weight_z3/ppermute | solution.py:39
  13.7 10.5 %collective-permute-start.5 = (bf16[16,32,256]{2,1,0:T(8,128)(2,1)}, bf16[16,32,256]{2,1,0:T(8,128)(2,1)S(1)}, u32[]{:S(2)}, u32[]{:S(2)}) collective-permute-start(bf16[16,32,256]{2,1,0:T(8,128)(2,1)} %get-tuple-element.33), channel_id=1, source_target_pairs={{8,24},{16,0},{9,25},{17,1},{10,26},{18,2},{11,27},{19,3},{12,28},... | collective-permute-start | bytes 786440 | tf_op jit(solution)/shard_map/around_first/ppermute | solution.py:45
  15.0 12.1 %collective-permute-start.4 = (bf16[16,32,256]{2,1,0:T(8,128)(2,1)}, bf16[16,32,256]{2,1,0:T(8,128)(2,1)S(1)}, u32[]{:S(2)}, u32[]{:S(2)}) collective-permute-start(bf16[16,32,256]{2,1,0:T(8,128)(2,1)} %get-tuple-element.32), channel_id=1, source_target_pairs={{0,8},{8,0},{16,24},{24,16},{1,9},{9,1},{17,25},{25,17},{2,10},{10... | collective-permute-start | bytes 786440 | tf_op jit(solution)/shard_map/cross/ppermute | solution.py:45
  19.4 4.9 %collective-permute-start.7 = (bf16[9,32,256]{2,1,0:T(8,128)(2,1)S(1)}, bf16[9,32,256]{2,1,0:T(8,128)(2,1)S(1)}, u32[]{:S(2)}, u32[]{:S(2)}) collective-permute-start(bf16[9,32,256]{2,1,0:T(8,128)(2,1)S(1)} %bitcast.19), channel_id=1, source_target_pairs={{0,1},{1,0},{2,3},{3,2},{4,5},{5,4},{6,7},{7,6},{8,9},{9,8},{10,11... | collective-permute-start | bytes 442376 | tf_op jit(solution)/shard_map/weight_core0/ppermute | solution.py:39
  19.4 4.9 %collective-permute-start.8 = (bf16[9,32,256]{2,1,0:T(8,128)(2,1)S(1)}, bf16[9,32,256]{2,1,0:T(8,128)(2,1)S(1)}, u32[]{:S(2)}, u32[]{:S(2)}) collective-permute-start(bf16[9,32,256]{2,1,0:T(8,128)(2,1)S(1)} %collective-permute-done.rest_1_), channel_id=1, source_target_pairs={{0,1},{1,0},{2,3},{3,2},{4,5},{5,4},{6,7},{7,6},{8,9},{9,8},{10,11... | collective-permute-start | bytes 442376 | tf_op jit(solution)/shard_map/weight_core1/ppermute | solution.py:39
  21.4 2.9 %collective-permute-start.10 = (bf16[9,32,256]{2,1,0:T(8,128)(2,1)S(1)}, bf16[9,32,256]{2,1,0:T(8,128)(2,1)S(1)}, u32[]{:S(2)}, u32[]{:S(2)}) collective-permute-start(bf16[9,32,256]{2,1,0:T(8,128)(2,1)S(1)} %collective-permute-done.6.rest_3_), channel_id=1, source_target_pairs={{0,1},{1,0},{2,3},{3,2},{4,5},{5,4},{6,7},{7,6},{8,9},{9,8},{10,11... | collective-permute-start | bytes 442376 | tf_op jit(solution)/shard_map/weight_core3/ppermute | solution.py:39
  28.6 2.1 %collective-permute-start.17 = (bf16[4,9,32,256]{3,2,1,0:T(8,128)(2,1)S(1)}, bf16[4,9,32,256]{3,2,1,0:T(8,128)(2,1)S(1)}, u32[]{:S(2)}, u32[]{:S(2)}) collective-permute-start(bf16[4,9,32,256]{3,2,1,0:T(8,128)(2,1)S(1)} %get-tuple-element.50), channel_id=1, source_target_pairs={{0,1},{1,0},{2,3},{3,2},{4,5},{5,4},{6,7},{7,6},{8,9},{9,8},{10,11... | collective-permute-start | bytes 1769480 | tf_op jit(solution)/shard_map/term_two/ppermute | solution.py:39
  28.7 12.2 %collective-permute-start.14 = (bf16[4,9,32,256]{3,2,1,0:T(8,128)(2,1)S(1)}, bf16[4,9,32,256]{3,2,1,0:T(8,128)(2,1)S(1)}, u32[]{:S(2)}, u32[]{:S(2)}) collective-permute-start(bf16[4,9,32,256]{3,2,1,0:T(8,128)(2,1)S(1)} %get-tuple-element.43), channel_id=1, source_target_pairs={{0,1},{1,0},{2,3},{3,2},{4,5},{5,4},{6,7},{7,6},{8,9},{9,8},{10,11... | collective-permute-start | bytes 1769480 | tf_op jit(solution)/shard_map/term_one/ppermute | solution.py:39
  29.2 26.3 %collective-permute-start.13 = (bf16[2,544,256]{2,1,0:T(8,128)(2,1)S(1)}, bf16[2,544,256]{2,1,0:T(8,128)(2,1)S(1)}, u32[]{:S(2)}, u32[]{:S(2)}) collective-permute-start(bf16[2,544,256]{2,1,0:T(8,128)(2,1)S(1)} %get-tuple-element.39.message), channel_id=1, source_target_pairs={{8,0},{16,8},{24,16},{9,1},{17,9},{25,17},{10,2},{18,10},{26,18},{... | collective-permute-start | bytes 1671176 | tf_op jit(solution)/shard_map/late_back/ppermute | solution.py:45
  31.3 12.1 %collective-permute-start.18 = (bf16[2,9,32,256]{3,2,1,0:T(8,128)(2,1)S(1)}, bf16[2,9,32,256]{3,2,1,0:T(8,128)(2,1)S(1)}, u32[]{:S(2)}, u32[]{:S(2)}) collective-permute-start(bf16[2,9,32,256]{3,2,1,0:T(8,128)(2,1)S(1)} %get-tuple-element.52), channel_id=1, source_target_pairs={{0,2},{1,3},{2,0},{3,1},{4,6},{5,7},{6,4},{7,5},{8,10},{9,11},{10,... | collective-permute-start | bytes 884744 | tf_op jit(solution)/shard_map/term_two_near/ppermute | solution.py:39
  32.1 15.7 %copy-start.3 = (bf16[2,1,16,32,256]{4,3,2,1,0:T(8,128)(2,1)S(1)}, bf16[2,1,16,32,256]{4,3,2,1,0:T(8,128)(2,1)}, u32[]{:S(2)}) copy-start(bf16[2,1,16,32,256]{4,3,2,1,0:T(8,128)(2,1)} %fresh.3) | copy-start | bytes 1572868
  32.1 15.7 %collective-permute-start.12 = (bf16[544,256]{1,0:T(8,128)(2,1)S(1)}, bf16[544,256]{1,0:T(8,128)(2,1)S(1)}, u32[]{:S(2)}, u32[]{:S(2)}) collective-permute-start(bf16[544,256]{1,0:T(8,128)(2,1)S(1)} %get-tuple-element.41.own_second), channel_id=1, source_target_pairs={{0,8},{8,16},{16,24},{1,9},{9,17},{17,25},{2,10},{10,18},{18,26},{... | collective-permute-start | bytes 835592 | tf_op jit(solution)/shard_map/late_fwd/ppermute | solution.py:45
  36.6 11.2 %collective-permute-start.11 = (bf16[16,32,256]{2,1,0:T(8,128)(2,1)S(1)}, bf16[16,32,256]{2,1,0:T(8,128)(2,1)S(1)}, u32[]{:S(2)}, u32[]{:S(2)}) collective-permute-start(bf16[16,32,256]{2,1,0:T(8,128)(2,1)S(1)} %collective-permute-done.5), channel_id=1, source_target_pairs={{0,8},{24,16},{1,9},{25,17},{2,10},{26,18},{3,11},{27,19},{4,12},{... | collective-permute-start | bytes 786440 | tf_op jit(solution)/shard_map/around_second/ppermute | solution.py:45
  41.6 11.3 %collective-permute-start.15 = (bf16[2,9,32,256]{3,2,1,0:T(8,128)(2,1)S(1)}, bf16[2,9,32,256]{3,2,1,0:T(8,128)(2,1)S(1)}, u32[]{:S(2)}, u32[]{:S(2)}) collective-permute-start(bf16[2,9,32,256]{3,2,1,0:T(8,128)(2,1)S(1)} %get-tuple-element.45), channel_id=1, source_target_pairs={{0,2},{1,3},{2,0},{3,1},{4,6},{5,7},{6,4},{7,5},{8,10},{9,11},{10,... | collective-permute-start | bytes 884744 | tf_op jit(solution)/shard_map/term_one_near/ppermute | solution.py:39
  44.1 9.6 %collective-permute-start.19 = (bf16[1,9,32,256]{3,2,1,0:T(8,128)(2,1)S(1)}, bf16[1,9,32,256]{3,2,1,0:T(8,128)(2,1)S(1)}, u32[]{:S(2)}, u32[]{:S(2)}) collective-permute-start(bf16[1,9,32,256]{3,2,1,0:T(8,128)(2,1)S(1)} %get-tuple-element.54), channel_id=1, source_target_pairs={{0,4},{1,5},{2,6},{3,7},{4,0},{5,1},{6,2},{7,3},{8,12},{9,13},{10,... | collective-permute-start | bytes 442376 | tf_op jit(solution)/shard_map/term_two_far/ppermute | solution.py:39
  53.4 7.3 %collective-permute-start.16 = (bf16[1,9,32,256]{3,2,1,0:T(8,128)(2,1)S(1)}, bf16[1,9,32,256]{3,2,1,0:T(8,128)(2,1)S(1)}, u32[]{:S(2)}, u32[]{:S(2)}) collective-permute-start(bf16[1,9,32,256]{3,2,1,0:T(8,128)(2,1)S(1)} %get-tuple-element.47), channel_id=1, source_target_pairs={{0,4},{1,5},{2,6},{3,7},{4,0},{5,1},{6,2},{7,3},{8,12},{9,13},{10,... | collective-permute-start | bytes 442376 | tf_op jit(solution)/shard_map/term_one_far/ppermute | solution.py:39
  54.2 7.7 %collective-permute-start.20 = (bf16[9,32,256]{2,1,0:T(8,128)(2,1)S(1)}, bf16[9,32,256]{2,1,0:T(8,128)(2,1)S(1)}, u32[]{:S(2)}, u32[]{:S(2)}) collective-permute-start(bf16[9,32,256]{2,1,0:T(8,128)(2,1)S(1)} %gather_sum_kernel.1), channel_id=1, source_target_pairs={{8,0},{16,8},{24,16},{9,1},{17,9},{25,17},{10,2},{18,10},{26,18},{... | collective-permute-start | bytes 442376 | tf_op jit(solution)/shard_map/below/ppermute | solution.py:45
